TPU v7x, 32 devices: a whole 2x2x4 slice. The times are simulated.
32 devices in a mesh: grp: 2 (over x), chan: 8 (over z, y), feed: 2 (over core).
Axes of the slice: x: 2, y: 2, z: 4, core: 2. Of those that a mesh axis runs over, the one named last changes fastest.
Arguments:
- voltages: int32 [2, 2048, 36608], P(None, ('grp', 'feed', 'chan')), parts along dimension 1, may hold values from -128 to 127, as said below
- input_order: int32 [1024], replicated, may hold values from 0 to 1023, each once
Outputs:
- visibility: float32 [2, 64, 1024, 1024], P(None, ('grp', 'chan'), 'feed'), parts along dimension 1
There are 2 independent parts, one for each index of `grp`. A program takes and returns all parts, laid end to end along the dimension named above; an argument that names none is the same for every part. Nothing has to cross between parts.
Inputs may be any that keep to these rules, and one draw needn't show every extreme that they name: `voltages`: 8-bit digitizer samples, saturated at the ends of the range. `input_order`: each input of 0 to 1023 stands exactly once.
All inputs are finite; a program needn't handle non-finite values.
Results may differ from a plain program's by a relative error of at most 0.0039.
Values may be sent and summed in bfloat16 or wider, within the bound.
No kernel may reach another device: no remote copies, remote signals or barrier semaphores. Data moves between devices by JAX's collectives and lax.ppermute only.
A program may use at most 192 MiB of HBM per device.

v0:
```python
import math

import jax
import jax.numpy as jnp
from jax import lax
from jax.sharding import PartitionSpec as P

CH = 256
TAPS = 16
AVG = 8


def swapped(block, axis, bit):
    count = lax.axis_size(axis)
    route = []
    for low in range(count):
        high = low | 1 << bit
        if high != low and high < count:
            route += [(low, high), (high, low)]
    return lax.ppermute(block, axis, route)


def make_window():
    length = TAPS * CH
    position = jnp.arange(length, dtype=jnp.float32) + 0.5
    profile = jnp.sinc((position - length / 2) / CH) * (
        0.5 - 0.5 * jnp.cos(2 * math.pi * position / length)
    )
    return profile.reshape(TAPS, CH)


def make_table():
    counter = jnp.arange(CH, dtype=jnp.int32)
    phases = counter[:, None] * counter[None, :] % CH
    angles = 2 * math.pi / CH * phases.astype(jnp.float32)
    cosine = jnp.cos(angles)
    sine_part = jnp.sin(angles)
    upper_rows = jnp.stack([cosine, -sine_part], axis=1)
    bottom = jnp.stack([sine_part, cosine], axis=1)
    return jnp.stack([upper_rows, bottom], axis=0).astype(jnp.bfloat16)


def polyphase(voltages, window):
    blocks = voltages.reshape(2, voltages.shape[1], -1, CH)
    frames = blocks.shape[2] - TAPS + 1
    running = window[0][None, None, None, :] * (
        blocks[:, :, 0:frames, :].astype(jnp.float32) / 64.0
    )
    for tap in range(1, TAPS):
        running = running + window[tap][None, None, None, :] * (
            blocks[:, :, tap : tap + frames, :].astype(jnp.float32) / 64.0
        )
    return running.astype(jnp.bfloat16)


def cross_products(left_rows, right_rows, norm_scale):
    twisted = jnp.stack(
        [left_rows, jnp.concatenate([left_rows[:, 1:2], -left_rows[:, 0:1]], axis=1)]
    )
    return (
        jnp.einsum("sarock,brock->soab", twisted, right_rows, preferred_element_type=jnp.float32)
        * norm_scale
    )


def body(voltages, input_order):
    window = make_window()
    table = make_table()
    filtered = polyphase(voltages, window)
    spectra = jnp.einsum("pftk,pkqm->fqmt", filtered, table, preferred_element_type=jnp.float32)
    spectra = (spectra * (1.0 / math.sqrt(CH))).astype(jnp.bfloat16)
    frames = spectra.shape[3]
    feed_rank = lax.axis_index("feed")
    is_first = feed_rank == 0
    received = lax.all_to_all(spectra, "chan", split_axis=2, concat_axis=0, tiled=True)
    partner = swapped(received, "feed", 0)
    all_feeds = jnp.where(
        is_first,
        jnp.concatenate([received, partner], axis=0),
        jnp.concatenate([partner, received], axis=0),
    )
    total_feeds = all_feeds.shape[0]
    chan_dev = all_feeds.shape[2]
    ordered = jnp.take(all_feeds, input_order, axis=0).reshape(
        total_feeds, 2, chan_dev // AVG, AVG, frames
    )
    norm_scale = 1.0 / (frames * AVG)
    half_count = total_feeds // 2
    own_rows = lax.dynamic_slice_in_dim(ordered, feed_rank * half_count, half_count, 0)
    result = cross_products(own_rows, ordered, norm_scale)
    return result


def solution(mesh):
    in_specs = (P(None, ("grp", "feed", "chan"), None), P())
    out_specs = P(None, ("grp", "chan"), "feed", None)
    return jax.shard_map(body, mesh=mesh, in_specs=in_specs, out_specs=out_specs, check_vma=False)
```

profile of v0, /device:TPU:0, one launch (start us, length us, event | category | flops | bytes accessed | tf_op | source)
XLA Modules:
  0.0 487.6 jit_solution(1667343619265333924)
XLA Ops:
  0.0 0.1 fusion.63
  0.1 1.0 fusion.58
  1.1 1.1 negate_convert_fusion
  2.2 19.4 %reshape.134 = s32[2,64,143,256]{3,2,1,0:T(8,128)} reshape(s32[2,64,36608]{2,1,0:T(8,128)} %param.2) | data formatting | bytes 37486592 | tf_op jit(solution)/shard_map/reshape | solution.py:44
  21.6 105.1 %fusion.100 = bf16[2,64,128,256,1]{3,2,0,1,4:T(8,128)(2,1)} fusion(s32[2,64,143,256]{3,2,1,0:T(8,128)} %reshape.134, f32[256]{0:T(256)S(1)} %get-tuple-element.10, f32[256]{0:T(256)S(1)} %get-tuple-element.11, f32[256]{0:T(256)S(1)} %get-tuple-element.12, f32[256]{0:T(256)S(1)} %get-tuple-element.13, f32[256]{0:T(256)S(1)} %get-tuple-element.14, ...), kind=kLoop, calls=%fused_computation.63.clone.clone.clone.2 | loop fusion | flops 201326592 | bytes 276840448 | tf_op jit(solution)/shard_map/pftk,pkqm->fqmt/dot_general | solution.py:70
  126.8 13.6 %fusion.43 = bf16[64,2,256,128]{3,2,0,1:T(8,128)(2,1)} fusion(bf16[1,256,2,256]{1,3,0,2:T(8,128)(2,1)S(1)} %get-tuple-element.8, bf16[1,256,2,256]{1,3,0,2:T(8,128)(2,1)S(1)} %get-tuple-element.7, bf16[2,64,128,256,1]{3,2,0,1,4:T(8,128)(2,1)} %fusion.100), kind=kOutput, calls=%fused_computation.60 | convolution fusion | flops 4304404480 | bytes 17301504 | tf_op jit(solution)/shard_map/pftk,pkqm->fqmt/dot_general | solution.py:70
  140.3 12.2 %copy.33 = bf16[64,2,256,128]{3,0,1,2:T(8,128)(2,1)} copy(bf16[64,2,256,128]{3,2,0,1:T(8,128)(2,1)} %fusion.43) | data formatting | bytes 16777216 | tf_op jit(solution)/shard_map/convert_element_type | solution.py:71
  152.5 0.0 copy-start
  152.5 190.7 %all_to_all.18 = bf16[64,2,256,128]{3,0,1,2:T(8,128)(2,1)} all-to-all(bf16[64,2,256,128]{3,0,1,2:T(8,128)(2,1)} %copy.33), channel_id=1, replica_groups=mesh['grp'=2,'chan'=8,'feed'=2] {'chan'}, dimensions={2} | all-to-all | bytes 16777216 | tf_op jit(solution)/shard_map/all_to_all | solution.py:75
  343.3 12.1 %copy.35 = bf16[8,64,2,32,128]{4,3,2,1,0:T(8,128)(2,1)} copy(bf16[8,64,2,32,128]{4,1,2,3,0:T(8,128)(2,1)} %bitcast.64) | data formatting | bytes 16777216 | tf_op jit(solution)/shard_map/all_to_all | solution.py:75
  355.4 0.0 collective-permute-start
  355.4 0.0 copy-done
  355.4 13.5 %collective-permute-done = bf16[512,2,32,128]{3,2,1,0:T(8,128)(2,1)} collective-permute-done((bf16[512,2,32,128]{3,2,1,0:T(8,128)(2,1)}, bf16[512,2,32,128]{3,2,1,0:T(8,128)(2,1)}, u32[]{:S(2)}, u32[]{:S(2)}) %collective-permute-start) | collective-permute-done | bytes 8388640 | tf_op jit(solution)/shard_map/ppermute | solution.py:20
  368.9 17.9 %maximum_select_fusion = bf16[1024,2,32,128]{3,2,1,0:T(8,128)(2,1)} fusion(bf16[512,2,32,128]{3,2,1,0:T(8,128)(2,1)} %collective-permute-done, bf16[512,2,32,128]{3,2,1,0:T(8,128)(2,1)} %bitcast.63, pred[]{:T(512)S(6)} %eq.111), kind=kLoop, calls=%fused_computation.49 | loop fusion | flops 25165824 | bytes 33554432 | tf_op jit(solution)/shard_map/jit(_where)/select_n | solution.py:77
  386.8 19.2 %gather_fusion = bf16[1024,2,32,128]{3,2,1,0:T(8,128)(2,1)} fusion(bf16[1024,2,32,128]{3,2,1,0:T(8,128)(2,1)} %maximum_select_fusion, s32[1024]{0:T(1024)S(1)} %fusion.88), kind=kCustom, calls=%fused_computation | custom fusion | bytes 33558528 | tf_op jit(solution)/shard_map/jit(_take)/gather | solution.py:84
  406.0 9.7 %copy.36 = bf16[1024,2,32,128]{3,0,1,2:T(8,128)(2,1)S(1)} copy(bf16[1024,2,32,128]{3,2,1,0:T(8,128)(2,1)} %gather_fusion) | data formatting | bytes 33554432 | tf_op jit(solution)/shard_map/jit(_take)/gather | solution.py:84
  415.7 7.2 %broadcast_select_fusion = bf16[1024,2,4,8,128]{4,0,1,3,2:T(8,128)(2,1)} fusion(bf16[1024,2,4,8,128]{4,0,1,3,2:T(8,128)(2,1)S(1)} %bitcast.61, pred[1024]{0:T(1024)(128)(4,1)S(1)} %compare_and_fusion), kind=kLoop, calls=%fused_computation.59 | loop fusion | flops 8388608 | bytes 33555456 | tf_op jit(solution)/shard_map/jit(_take)/select_n | solution.py:84
  422.9 7.6 %dynamic-slice_bitcast_fusion = bf16[1,512,2,4,8,128]{5,1,2,4,0,3:T(8,128)(2,1)} fusion(bf16[1024,2,4,8,128]{4,0,1,3,2:T(8,128)(2,1)} %broadcast_select_fusion, s32[]{:T(128)S(6)} %select_n.231), kind=kLoop, calls=%fused_computation.65 | loop fusion | bytes 16777220 | tf_op jit(solution)/shard_map/stack | solution.py:57
  430.5 6.8 %constant_dynamic-slice_fusion = (bf16[512,1,4,8,128]{4,0,1,3,2:T(8,128)(2,1)S(1)}, bf16[512,1,4,8,128]{4,0,1,3,2:T(8,128)(2,1)}) fusion(bf16[1024,2,4,8,128]{4,0,1,3,2:T(8,128)(2,1)} %broadcast_select_fusion, s32[]{:T(128)S(6)} %select_n.231, s32[]{:T(128)S(6)} %add.414), kind=kLoop, calls=%fused_computation.141 | loop fusion | flops 6291456 | bytes 16777224 | tf_op jit(solution)/shard_map/slice | solution.py:58
  437.3 6.2 %maximum_bitcast_fusion = bf16[1,512,2,4,8,128]{5,1,2,4,0,3:T(8,128)(2,1)} fusion(bf16[512,1,4,8,128]{4,0,1,3,2:T(8,128)(2,1)} %get-tuple-element.6, bf16[512,1,4,8,128]{4,0,1,3,2:T(8,128)(2,1)S(1)} %get-tuple-element.5), kind=kLoop, calls=%fused_computation.61 | loop fusion | flops 4194304 | bytes 16777216 | tf_op jit(solution)/shard_map/stack | solution.py:57
  443.5 27.6 %fusion.36 = f32[2,4,512,1024]{2,3,0,1:T(8,128)} fusion(bf16[1,512,2,4,8,128]{5,1,2,4,0,3:T(8,128)(2,1)} %maximum_bitcast_fusion, bf16[1,512,2,4,8,128]{5,1,2,4,0,3:T(8,128)(2,1)} %dynamic-slice_bitcast_fusion, bf16[1024,2,4,8,128]{4,0,1,3,2:T(8,128)(2,1)} %broadcast_select_fusion), kind=kOutput, calls=%fused_computation.55 | convolution fusion | flops 17217617920 | bytes 50331648 | tf_op jit(solution)/shard_map/sarock,brock->soab/dot_general | solution.py:61
  471.2 16.4 %copy.37 = f32[2,4,512,1024]{3,2,1,0:T(8,128)} copy(f32[2,4,512,1024]{2,3,0,1:T(8,128)} %fusion.36) | data formatting | bytes 33554432 | tf_op jit(solution)/shard_map/mul | solution.py:61
  (4 shorter events, 0.1 us)
Async XLA Ops:
  152.5 202.8 %copy-start = (s32[1024]{0:T(1024)S(1)}, s32[1024]{0:T(1024)}, u32[]{:S(2)}) copy-start(s32[1024]{0:T(1024)} %param.3) | copy-start | bytes 12292
  355.4 13.5 %collective-permute-start = (bf16[512,2,32,128]{3,2,1,0:T(8,128)(2,1)}, bf16[512,2,32,128]{3,2,1,0:T(8,128)(2,1)}, u32[]{:S(2)}, u32[]{:S(2)}) collective-permute-start(bf16[512,2,32,128]{3,2,1,0:T(8,128)(2,1)} %bitcast.62), channel_id=1, source_target_pairs={{0,1},{1,0},{2,3},{3,2},{4,5},{5,4},{6,7},{7,6},{8,9},{9,8},{10,11... | collective-permute-start | bytes 25165832 | tf_op jit(solution)/shard_map/ppermute | solution.py:20
where the time goes:
time: 489 us; the launch traced here: 488 us
  blocking collectives  191 us (39%)
  other arithmetic  146 us (30%)
  local copies, waits for them, and re-layouts  96.6 us (20%)
  matrix products  41.2 us (8%)
  waiting for transfers between devices  13.5 us (3%)
    all_to_all x1, blocking collectives, body(): lax.all_to_all(spectra, 'chan', split_axis=2, concat_axis=0, tiled=True)  191 us
    dot_general x1, other arithmetic, body(): jnp.einsum('pftk,pkqm->fqmt', filtered, table, preferred_element_type=jnp...  105 us
    gather x2, local copies, waits for them, and re-layouts, body(): jnp.take(all_feeds, input_order, axis=0)  28.9 us
    dot_general x1, matrix products, cross_products(): jnp.einsum('sarock,brock->soab', twisted, right_rows, preferred_element_t...  27.6 us
    reshape x1, local copies, waits for them, and re-layouts, polyphase(): blocks = voltages.reshape(2, voltages.shape[1], -1, CH)  19.4 us
    select_n x1, other arithmetic, body(): jnp.where(is_first, jnp.concatenate([received, partner], axis=0), jnp.con...  17.9 us
    mul x1, local copies, waits for them, and re-layouts, cross_products(): jnp.einsum('sarock,brock->soab', twisted, right_rows, preferred_element_t...  16.4 us
    dot_general x1, matrix products, body(): jnp.einsum('pftk,pkqm->fqmt', filtered, table, preferred_element_type=jnp...  13.6 us
  transfers between devices with their start and end apart: 1, of which 1 were waited for; matrix products, arithmetic and copies ran while one was open for 0% of the time, Pallas kernels for 0%

commit v1 on v0

v1 whole, which is shorter than its diff:
```python
import functools
import math

import jax
import jax.numpy as jnp
import numpy as np
from jax import lax
from jax.experimental import pallas as pl
from jax.experimental.pallas import tpu as pltpu
from jax.sharding import PartitionSpec as P

CH = 256
TAPS = 16
AVG = 8
LANES = 128
STEP = 16
COLS = 256
VMEM = 60 * 1024 * 1024
WINDOW = 5
NT = (((1,), (1,)), ((), ()))


def make_window():
    length = TAPS * CH
    position = np.arange(length, dtype=np.float64) + 0.5
    profile = np.sinc((position - length / 2) / CH) * (
        0.5 - 0.5 * np.cos(2 * math.pi * position / length)
    )
    profile = profile.astype(np.float32).reshape(TAPS, 1, CH) / np.float32(64 * math.sqrt(CH))
    return np.ascontiguousarray(np.broadcast_to(profile, (TAPS, 8, CH)))


def make_table():
    counter = np.arange(CH)
    angles = 2 * math.pi / CH * (counter[:, None] * counter[None, :] % CH)
    cosine, sine = np.cos(angles), np.sin(angles)
    table = np.stack(
        [np.concatenate([cosine, sine], axis=1), np.concatenate([-sine, cosine], axis=1)]
    )
    table = table.reshape(2, CH // AVG, AVG, 2 * CH).transpose(1, 0, 2, 3)
    return table.reshape(2 * CH, 2 * CH).astype(np.float32).astype(jnp.bfloat16)


def channelize_kernel(sizes, me_ref, va_ref, vb_ref, win_ref, tab_ref, *rest):
    feeds, chans, outs_per_dev, groups = sizes
    outs, (tabs, filt) = rest[:-2], rest[-2:]
    me = me_ref[0]
    span = LANES // feeds
    part = 2 * AVG * outs_per_dev

    @pl.when(pl.program_id(0) == 0)
    def _():
        for k in range(chans):
            start = pl.multiple_of((me ^ k) * part, part)
            tabs[k * part : (k + 1) * part, :] = tab_ref[pl.ds(start, part), :]

    flip = lax.rem(me, span)

    def strip(index, carry):
        f0 = pl.multiple_of(index * 16, 16)
        for p in range(2):
            for kk in range(CH // LANES):
                lanes = slice(kk * LANES, (kk + 1) * LANES)
                weights = [win_ref[tap, :, lanes] for tap in range(TAPS)]
                for t0 in range(0, STEP, 8):
                    total = [[None] * 8, [None] * 8]
                    for u in range(t0, t0 + 8 + TAPS - 1):
                        src = va_ref if u < STEP else vb_ref
                        col = (u % STEP) * CH + kk * LANES
                        both = src[p, pl.ds(f0, 16), col : col + LANES].astype(jnp.float32)
                        for half in range(2):
                            x = both[half * 8 : half * 8 + 8]
                            for t in range(8):
                                tap = u - t0 - t
                                if 0 <= tap < TAPS:
                                    term = weights[tap] * x
                                    old = total[half][t]
                                    total[half][t] = term if old is None else old + term
                    for t in range(8):
                        slot = ((t0 + t) // span) * span + ((t0 + t) % span ^ flip)
                        row = pl.multiple_of(slot * feeds + f0, 16)
                        value = jnp.concatenate([total[0][t], total[1][t]], axis=0)
                        filt[pl.ds(row, 16), p * CH + kk * LANES : p * CH + (kk + 1) * LANES] = (
                            value.astype(jnp.bfloat16)
                        )
        return carry

    lax.fori_loop(0, feeds // 16, strip, 0)

    for c in range(STEP * feeds // 256):
        product = lax.dot_general(
            tabs[...], filt[c * 256 : (c + 1) * 256, :], NT, preferred_element_type=jnp.float32
        )
        product = product.reshape(2 * CH // AVG, AVG, 256)
        packed = jnp.concatenate([product[:, :, :LANES], product[:, :, LANES:]], axis=1)
        packed = packed.astype(jnp.bfloat16).reshape(chans, outs_per_dev, 2, 2 * AVG, LANES)
        for k in range(chans):
            for g, (first, count) in enumerate(groups):
                outs[g * chans + k][:, :, c] = packed[k, first : first + count]


def channelize(voltages, me, window, table, first, steps, groups, chans):
    feeds = voltages.shape[1]
    outs_per_dev = CH // chans // AVG
    blocks = STEP * feeds // 256
    out_shape, out_specs = [], []
    for _, count in groups:
        for _ in range(chans):
            out_shape.append(
                jax.ShapeDtypeStruct((count, 2, steps * blocks, 2 * AVG, LANES), jnp.bfloat16)
            )
            out_specs.append(
                pl.BlockSpec((count, 2, blocks, 2 * AVG, LANES), lambda i, me: (0, 0, i, 0, 0))
            )
    block = (2, feeds, STEP * CH)
    rows = steps * STEP * feeds
    result = pl.pallas_call(
        functools.partial(channelize_kernel, (feeds, chans, outs_per_dev, groups)),
        grid_spec=pltpu.PrefetchScalarGridSpec(
            num_scalar_prefetch=1,
            grid=(steps,),
            in_specs=[
                pl.BlockSpec(block, lambda i, me: (0, 0, first + i)),
                pl.BlockSpec(block, lambda i, me: (0, 0, first + i + 1)),
                pl.BlockSpec((TAPS, 8, CH), lambda i, me: (0, 0, 0)),
                pl.BlockSpec((2 * CH, 2 * CH), lambda i, me: (0, 0)),
            ],
            out_specs=out_specs,
            scratch_shapes=[
                pltpu.VMEM((2 * CH, 2 * CH), jnp.bfloat16),
                pltpu.VMEM((STEP * feeds, 2 * CH), jnp.bfloat16),
            ],
        ),
        out_shape=out_shape,
        compiler_params=pltpu.CompilerParams(vmem_limit_bytes=VMEM),
        cost_estimate=pl.CostEstimate(
            flops=rows * (4 * CH * CH * 2 + 64 * CH * TAPS),
            bytes_accessed=steps * 2 * 2 * feeds * STEP * CH * 4 + rows * 4 * CH,
            transcendentals=0,
        ),
    )(me.reshape(1), voltages, voltages, window, table)
    return [result[g * chans : (g + 1) * chans] for g in range(len(groups))]


def correlate_kernel(sizes, feed_ref, *refs):
    feeds, chans, pieces, norm_scale = sizes
    own = refs[0 : 2 * pieces : 2]
    partner = refs[1 : 2 * pieces : 2]
    select = refs[2 * pieces]
    out_ref, rows_ref = refs[-2:]
    span = LANES // feeds
    inputs = select.shape[1]
    depth = rows_ref.shape[1] // 2

    @pl.when(pl.program_id(1) == 0)
    def _():
        low = lax.broadcasted_iota(jnp.int32, (256, LANES), 1) // feeds
        base = 0
        for piece in range(pieces):
            lines = own[piece].shape[3] * 16
            for x in range(span):
                for first in range(0, 2 * lines, 256):
                    tiles = []
                    for ref in (own[piece], partner[piece]):
                        for j in range(chans // span):
                            tile = None
                            for slot in range(span):
                                source = ref[j * span + (slot ^ x), 0].reshape(2 * lines, LANES)
                                source = source[first : first + 256]
                                tile = source if tile is None else jnp.where(low == slot, source, tile)
                            tiles.append(tile)
                    value = lax.dot_general(
                        select[x],
                        jnp.concatenate(tiles, axis=1),
                        NT,
                        preferred_element_type=jnp.float32,
                    ).astype(jnp.bfloat16)
                    start = first
                    while start < first + 256:
                        q, line = start // lines, start % lines
                        count = min(lines - line, first + 256 - start)
                        place = q * depth + base + line
                        rows_ref[:, place : place + count] = value[
                            :, start - first : start - first + count
                        ]
                        start += count
                base += lines

    half = out_ref.shape[2]
    mine = pl.ds(pl.multiple_of(feed_ref[0] * half, half), half)
    start = pl.multiple_of(pl.program_id(1) * COLS, COLS)
    other = pl.ds(start, COLS)

    def dot(left, right):
        return lax.dot_general(left, right, NT, preferred_element_type=jnp.float32)

    real, imag = slice(0, depth), slice(depth, 2 * depth)
    out_ref[0, 0] = dot(rows_ref[mine, :], rows_ref[other, :]) * norm_scale
    out_ref[1, 0] = (
        dot(rows_ref[mine, imag], rows_ref[other, real])
        - dot(rows_ref[mine, real], rows_ref[other, imag])
    ) * norm_scale


def correlate(feed, pieces, select, first, count, out_count, frames, feeds, chans, result):
    span, total, inputs = select.shape
    half = total // 2
    operands, in_specs = [], []
    depth = 0
    for own, partner, place in pieces:
        block = (chans, 1) + own.shape[2:]
        for array in (own, partner):
            operands.append(array)
            in_specs.append(
                pl.BlockSpec(
                    block,
                    functools.partial(lambda place, o, n, feed: (0, place + o, 0, 0, 0, 0), place),
                )
            )
        depth += own.shape[3] * 16 * span
    operands.append(select)
    in_specs.append(
        pl.BlockSpec(select.shape, lambda o, n, feed: (0, 0, 0), pipeline_mode=pl.Buffered(1))
    )
    aliases = {}
    if result is not None:
        aliases = {1 + len(operands): 0}
        operands.append(result)
        in_specs.append(pl.BlockSpec(memory_space=pl.ANY))
    return pl.pallas_call(
        functools.partial(correlate_kernel, (feeds, chans, len(pieces), 1.0 / (frames * AVG))),
        grid_spec=pltpu.PrefetchScalarGridSpec(
            num_scalar_prefetch=1,
            grid=(count, total // COLS),
            in_specs=in_specs,
            out_specs=pl.BlockSpec((2, 1, half, COLS), lambda o, n, feed: (0, first + o, 0, n)),
            scratch_shapes=[pltpu.VMEM((total, 2 * depth), jnp.bfloat16)],
        ),
        out_shape=jax.ShapeDtypeStruct((2, out_count, half, total), jnp.float32),
        input_output_aliases=aliases,
        compiler_params=pltpu.CompilerParams(vmem_limit_bytes=40 * 1024 * 1024),
        cost_estimate=pl.CostEstimate(flops=1000, bytes_accessed=1000, transcendentals=0),
    )(feed.reshape(1), *operands)


def body(voltages, input_order):
    feeds = voltages.shape[1]
    chans = lax.axis_size("chan")
    me = lax.axis_index("chan").astype(jnp.int32)
    feed = lax.axis_index("feed").astype(jnp.int32)
    frames = voltages.shape[2] // CH - TAPS + 1
    steps = frames // STEP
    outs_per_dev = CH // chans // AVG
    span = LANES // feeds
    window = jnp.asarray(make_window())
    table = jnp.asarray(make_table())

    k = jnp.arange(chans, dtype=jnp.int32)
    k = (k[None, :] // span) * span + ((k[None, :] % span) ^ jnp.arange(span, dtype=jnp.int32)[:, None])
    sources = (
        ((feed ^ jnp.arange(2, dtype=jnp.int32)) * (chans * feeds))[None, :, None, None]
        + ((me ^ k) * feeds)[:, None, :, None]
        + jnp.arange(feeds, dtype=jnp.int32)[None, None, None, :]
    ).reshape(span, 1, 2 * chans * feeds)
    select = (input_order[None, :, None] == sources).astype(jnp.bfloat16)

    near, far = range(1, chans // 2), range(chans // 2, chans)
    turns = [k for pair in zip(far, near) for k in pair] + [chans - 1]
    flying = []

    def send(blocks, order):
        received = {}
        for k in order:
            block = blocks[k]
            if len(flying) >= WINDOW:
                store, key = flying.pop(0)
                block, store[key] = lax.optimization_barrier((block, store[key]))
            received[k] = lax.ppermute(block, "chan", [(c, c ^ k) for c in range(chans)])
            flying.append((received, k))
        return received

    def share(block, received, result):
        if result is not None:
            received[1], result = lax.optimization_barrier((received[1], result))
        own = jnp.stack([block] + [received[k] for k in range(1, chans)])
        return (own, lax.ppermute(own, "feed", [(0, 1), (1, 0)])), result

    unit = LANES // feeds
    groups = [(0, outs_per_dev)]
    if outs_per_dev > 1:
        groups = [(0, outs_per_dev - 1), (outs_per_dev - 1, 1)]
    pieces = []
    if steps > unit:
        blocks = channelize(voltages, me, window, table, 0, unit, [(0, outs_per_dev)], chans)[0]
        blocks = list(blocks)
        pieces.append((blocks[0], send(blocks, turns)))
        me, blocks[0] = lax.optimization_barrier((me, blocks[0]))
        pieces[0] = (blocks[0], pieces[0][1])
        first = unit
    else:
        first = 0
    blocks = channelize(voltages, me, window, table, first, steps - first, groups, chans)
    sent = [send(group, turns) for group in blocks[:-1]]
    sent.append(send(blocks[-1], [*far, *near]))
    result = None
    shared = [share(block, received, None)[0] for block, received in pieces]
    for group, received, (first, count) in zip(blocks, sent, groups):
        block, result = share(group[0], received, result)
        result = correlate(
            feed, [piece + (first,) for piece in shared] + [block + (0,)],
            select, first, count, outs_per_dev, frames, feeds, chans, result,
        )
    return result


def solution(mesh):
    in_specs = (P(None, ("grp", "feed", "chan"), None), P())
    out_specs = P(None, ("grp", "chan"), "feed", None)
    return jax.shard_map(body, mesh=mesh, in_specs=in_specs, out_specs=out_specs, check_vma=False)
```

time: 489 us -> 247 us (0.51)
  blocking collectives: 191 us -> 0 us
  other arithmetic: 146 us -> 0.84 us
  local copies, waits for them, and re-layouts: 96.6 us -> 9.48 us
  Pallas kernels: 0 us -> 80.1 us
  starting transfers between devices: 0.01 us -> 76.2 us
  waiting for transfers between devices: 13.5 us -> 79.9 us
  matrix products: 41.2 us -> 0 us
    all_to_all x1 -> x0, blocking collectives: 191 us -> none  [body(): lax.all_to_all(spectra, 'chan', split_axis=2, concat_axis=0, tiled=True)]
    dot_general x1 -> x0, other arithmetic: 105 us -> none  [body(): jnp.einsum('pftk,pkqm->fqmt', filtered, table, preferred_element_type=jnp...]
    pallas_call x0 -> x4, Pallas kernels: none -> 80.1 us  [the longest x2 47.5 us: correlate(): pl.pallas_call(functools.partial(correlate_kernel, (feeds, chans, len(pie...]
    ppermute x1 -> x24, starting transfers between devices: 0.01 us -> 76.2 us  [the longest x21 75.5 us: send(): lax.ppermute(block, 'chan', [(c, c ^ k) for c in range(chans)])]
    ppermute x1 -> x24, waiting for transfers between devices: 13.5 us -> 79.9 us  [the longest x21 76.5 us: send(): lax.ppermute(block, 'chan', [(c, c ^ k) for c in range(chans)])]
    dot_general x2 -> x0, matrix products: 41.2 us -> none  [the longest x1 27.6 us: cross_products(): jnp.einsum('sarock,brock->soab', twisted, right_rows, preferred_element_t...]
    gather x2 -> x0, local copies, waits for them, and re-layouts: 28.9 us -> none  [body(): jnp.take(all_feeds, input_order, axis=0)]
    select_n x2 -> x1, other arithmetic: 25.1 us -> 0.01 us  [body(): k[None, :] % span]
  transfers between devices with their start and end apart: 1 -> 24, of which waited for: 1 -> 8; matrix products, arithmetic and copies ran while one was open for 0% -> 2% of each run, Pallas kernels for 0% -> 24%
where the time goes in v1:
time: 247 us
  Pallas kernels  80.1 us (32%)
  waiting for transfers between devices  79.9 us (32%)
  starting transfers between devices  76.2 us (31%)
  local copies, waits for them, and re-layouts  9.48 us (4%)
    ppermute x21, waiting for transfers between devices, send(): lax.ppermute(block, 'chan', [(c, c ^ k) for c in range(chans)])  76.5 us
    ppermute x21, starting transfers between devices, send(): lax.ppermute(block, 'chan', [(c, c ^ k) for c in range(chans)])  75.5 us
    pallas_call x2, Pallas kernels, correlate(): pl.pallas_call(functools.partial(correlate_kernel, (feeds, chans, len(pie...  47.5 us
    pallas_call x2, Pallas kernels, channelize(): pl.pallas_call(functools.partial(channelize_kernel, (feeds, chans, outs_p...  32.7 us
    unnamed x45, local copies, waits for them, and re-layouts  8.26 us
  transfers between devices with their start and end apart: 24, of which 8 were waited for; matrix products, arithmetic and copies ran while one was open for 2% of the time, Pallas kernels for 24%

profile of v1, /device:TPU:0, one launch (start us, length us, event | category | flops | bytes accessed | tf_op | source)
XLA Modules:
  0.0 246.8 jit_solution(10715512971985357980)
XLA Ops:
  0.0 9.7 %shard_map.46 = (bf16[4,2,8,16,128]{4,3,2,1,0:T(8,128)(2,1)}, bf16[4,2,8,16,128]{4,3,2,1,0:T(8,128)(2,1)}, bf16[4,2,8,16,128]{4,3,2,1,0:T(8,128)(2,1)}, bf16[4,2...) custom-call(s32[1]{0:T(128)} %bitcast.1.me_ref, ...), custom_call_target="tpu_custom_call" | custom-call | flops 1610612736 | bytes 10485760 | tf_op jit(solution)/shard_map/pallas_call | solution.py:117
  9.7 3.0 %collective-permute-start = (bf16[4,2,8,16,128]{4,3,2,1,0:T(8,128)(2,1)}, bf16[4,2,8,16,128]{4,3,2,1,0:T(8,128)(2,1)S(1)}, u32[]{:S(2)}, u32[]{:S(2)}) collective-permute-start(bf16[4,2,8,16,128]{4,3,2,1,0:T(8,128)(2,1)} %get-tuple-element.68), channel_id=1, source_target_pairs={{0,2},{2,0},{4,6},{6,4},{8,10},{10,8},{12,14},{14,12},{1,3},{3,1},... | collective-permute-start | bytes 786440 | tf_op jit(solution)/shard_map/ppermute | solution.py:278
  12.7 1.6 collective-permute-start.1
  14.3 2.6 %collective-permute-start.2 = (bf16[4,2,8,16,128]{4,3,2,1,0:T(8,128)(2,1)}, bf16[4,2,8,16,128]{4,3,2,1,0:T(8,128)(2,1)S(1)}, u32[]{:S(2)}, u32[]{:S(2)}) collective-permute-start(bf16[4,2,8,16,128]{4,3,2,1,0:T(8,128)(2,1)} %get-tuple-element.76), channel_id=1, source_target_pairs={{0,8},{2,10},{4,12},{6,14},{8,0},{10,2},{12,4},{14,6},{1,9},{3,11}... | collective-permute-start | bytes 786440 | tf_op jit(solution)/shard_map/ppermute | solution.py:278
  17.2 2.5 %collective-permute-start.5 = (bf16[4,2,8,16,128]{4,3,2,1,0:T(8,128)(2,1)}, bf16[4,2,8,16,128]{4,3,2,1,0:T(8,128)(2,1)S(1)}, u32[]{:S(2)}, u32[]{:S(2)}) collective-permute-start(bf16[4,2,8,16,128]{4,3,2,1,0:T(8,128)(2,1)} %get-tuple-element.84), channel_id=1, source_target_pairs={{0,12},{2,14},{4,8},{6,10},{8,4},{10,6},{12,0},{14,2},{1,13},{3,15... | collective-permute-start | bytes 786440 | tf_op jit(solution)/shard_map/ppermute | solution.py:278
  19.7 23.0 %shard_map.47 = (bf16[3,2,24,16,128]{4,3,2,1,0:T(8,128)(2,1)}, bf16[3,2,24,16,128]{4,3,2,1,0:T(8,128)(2,1)}, bf16[3,2,24,16,128]{4,3,2,1,0:T(8,128)(2,1)}, bf16[...) custom-call(s32[1]{0:T(128)} %bitcast.4.me_ref, ...), custom_call_target="tpu_custom_call" | custom-call | flops 4831838208 | bytes 31457280 | tf_op jit(solution)/shard_map/pallas_call | solution.py:117
  42.6 4.4 %collective-permute-done.4 = bf16[4,2,8,16,128]{4,3,2,1,0:T(8,128)(2,1)S(1)} collective-permute-done((bf16[4,2,8,16,128]{4,3,2,1,0:T(8,128)(2,1)}, bf16[4,2,8,16,128]{4,3,2,1,0:T(8,128)(2,1)S(1)}, u32[]{:S(2)}, u32[]{:S(2)}) %collective-permute-start.4) | collective-permute-done | bytes 262176 | tf_op jit(solution)/shard_map/ppermute | solution.py:278
  48.6 17.1 %collective-permute-start.6 = (bf16[4,2,8,16,128]{4,3,2,1,0:T(8,128)(2,1)S(1)}, bf16[4,2,8,16,128]{4,3,2,1,0:T(8,128)(2,1)S(1)}, u32[]{:S(2)}, u32[]{:S(2)}) collective-permute-start(bf16[4,2,8,16,128]{4,3,2,1,0:T(8,128)(2,1)S(1)} %copy-done.4), channel_id=1, source_target_pairs={{0,14},{2,12},{4,10},{6,8},{8,6},{10,4},{12,2},{14,0},{1,15},{3,13... | collective-permute-start | bytes 786440 | tf_op jit(solution)/shard_map/ppermute | solution.py:278
  66.4 3.3 %collective-permute-start.14 = (bf16[3,2,24,16,128]{4,3,2,1,0:T(8,128)(2,1)}, bf16[3,2,24,16,128]{4,3,2,1,0:T(8,128)(2,1)S(1)}, u32[]{:S(2)}, u32[]{:S(2)}) collective-permute-start(bf16[3,2,24,16,128]{4,3,2,1,0:T(8,128)(2,1)} %get-tuple-element.107), channel_id=1, source_target_pairs={{0,10},{2,8},{4,14},{6,12},{8,2},{10,0},{12,6},{14,4},{1,11},{3,9}... | collective-permute-start | bytes 1769480 | tf_op jit(solution)/shard_map/ppermute | solution.py:278
  69.7 14.8 %collective-permute-done.6 = bf16[4,2,8,16,128]{4,3,2,1,0:T(8,128)(2,1)S(1)} collective-permute-done((bf16[4,2,8,16,128]{4,3,2,1,0:T(8,128)(2,1)S(1)}, bf16[4,2,8,16,128]{4,3,2,1,0:T(8,128)(2,1)S(1)}, u32[]{:S(2)}, u32[]{:S(2)}) %collective-permute-start.6) | collective-permute-done | bytes 262176 | tf_op jit(solution)/shard_map/ppermute | solution.py:278
  84.5 32.1 %collective-permute-start.11 = (bf16[3,2,24,16,128]{4,3,2,1,0:T(8,128)(2,1)}, bf16[3,2,24,16,128]{4,3,2,1,0:T(8,128)(2,1)S(1)}, u32[]{:S(2)}, u32[]{:S(2)}) collective-permute-start(bf16[3,2,24,16,128]{4,3,2,1,0:T(8,128)(2,1)} %get-tuple-element.98), channel_id=1, source_target_pairs={{0,4},{2,6},{4,0},{6,2},{8,12},{10,14},{12,8},{14,10},{1,5},{3,7},... | collective-permute-start | bytes 1769480 | tf_op jit(solution)/shard_map/ppermute | solution.py:278
  119.0 2.0 bitcast_dynamic-update-slice_fusion.7
  121.0 6.1 %collective-permute-done.14 = bf16[3,2,24,16,128]{4,3,2,1,0:T(8,128)(2,1)S(1)} collective-permute-done((bf16[3,2,24,16,128]{4,3,2,1,0:T(8,128)(2,1)}, bf16[3,2,24,16,128]{4,3,2,1,0:T(8,128)(2,1)S(1)}, u32[]{:S(2)}, u32[]{:S(2)}) %collective-permute-start.14) | collective-permute-done | bytes 589856 | tf_op jit(solution)/shard_map/ppermute | solution.py:278
  128.1 12.5 %collective-permute-done.11 = bf16[3,2,24,16,128]{4,3,2,1,0:T(8,128)(2,1)S(1)} collective-permute-done((bf16[3,2,24,16,128]{4,3,2,1,0:T(8,128)(2,1)}, bf16[3,2,24,16,128]{4,3,2,1,0:T(8,128)(2,1)S(1)}, u32[]{:S(2)}, u32[]{:S(2)}) %collective-permute-start.11) | collective-permute-done | bytes 589856 | tf_op jit(solution)/shard_map/ppermute | solution.py:278
  141.5 21.8 %collective-permute-done.13 = bf16[3,2,24,16,128]{4,3,2,1,0:T(8,128)(2,1)S(1)} collective-permute-done((bf16[3,2,24,16,128]{4,3,2,1,0:T(8,128)(2,1)}, bf16[3,2,24,16,128]{4,3,2,1,0:T(8,128)(2,1)S(1)}, u32[]{:S(2)}, u32[]{:S(2)}) %collective-permute-start.13) | collective-permute-done | bytes 589856 | tf_op jit(solution)/shard_map/ppermute | solution.py:278
  170.3 1.6 collective-permute-start.17
  171.9 2.0 collective-permute-start.19
  174.7 11.9 %collective-permute-done.17 = bf16[1,2,24,16,128]{4,3,2,1,0:T(8,128)(2,1)S(1)} collective-permute-done((bf16[1,2,24,16,128]{4,3,2,1,0:T(8,128)(2,1)S(1)}, bf16[1,2,24,16,128]{4,3,2,1,0:T(8,128)(2,1)S(1)}, u32[]{:S(2)}, u32[]{:S(2)}) %collective-permute-start.17) | collective-permute-done | bytes 196640 | tf_op jit(solution)/shard_map/ppermute | solution.py:278
  186.6 4.9 %collective-permute-done.19 = bf16[1,2,24,16,128]{4,3,2,1,0:T(8,128)(2,1)S(1)} collective-permute-done((bf16[1,2,24,16,128]{4,3,2,1,0:T(8,128)(2,1)S(1)}, bf16[1,2,24,16,128]{4,3,2,1,0:T(8,128)(2,1)S(1)}, u32[]{:S(2)}, u32[]{:S(2)}) %collective-permute-start.19) | collective-permute-done | bytes 196640 | tf_op jit(solution)/shard_map/ppermute | solution.py:278
  191.5 1.9 collective-permute-start.21
  193.4 2.1 collective-permute-start.22
  195.6 35.6 %shard_map.48.refs_5_ = f32[2,4,512,1024]{3,2,1,0:T(8,128)} custom-call(s32[1]{0:T(128)} %bitcast.feed_ref, bf16[8,4,2,8,16,128]{5,4,3,2,1,0:T(8,128)(2,1)S(1)} %bitcast_dynamic-update-slice_fusion.8.refs_0_, bf16[8,4,2,8,16,128]{5,4,3,2,1,0:T(8,128)(2,1)} %collective-permute-done.7.refs_1_, ...), custom_call_target="tpu_custom_call" | custom-call | flops 1000 | bytes 1000 | tf_op jit(solution)/shard_map/pallas_call | solution.py:230
  231.6 3.4 %collective-permute-done.23.refs_3_ = bf16[8,1,2,24,16,128]{5,4,3,2,1,0:T(8,128)(2,1)S(1)} collective-permute-done((bf16[8,1,2,24,16,128]{5,4,3,2,1,0:T(8,128)(2,1)S(1)}, bf16[8,1,2,24,16,128]{5,4,3,2,1,0:T(8,128)(2,1)S(1)}, u32[]{:S(2)}, u32[]{:S(2)}) %collective-permute-start.23) | collective-permute-done | bytes 1572896 | tf_op jit(solution)/shard_map/ppermute | solution.py:286
  235.0 11.9 %shard_map.49 = f32[2,4,512,1024]{3,2,1,0:T(8,128)} custom-call(s32[1]{0:T(128)} %bitcast.feed_ref, bf16[8,4,2,8,16,128]{5,4,3,2,1,0:T(8,128)(2,1)S(1)} %bitcast_dynamic-update-slice_fusion.8.refs_0_, bf16[8,4,2,8,16,128]{5,4,3,2,1,0:T(8,128)(2,1)} %collective-permute-done.7.refs_1_, ...), custom_call_target="tpu_custom_call", output_to_operand_aliasing={{}: (6, {})} | custom-call | flops 1000 | bytes 1000 | tf_op jit(solution)/shard_map/pallas_call | solution.py:230
  (86 shorter events, 14.5 us)
Async XLA Ops:
  9.7 38.9 %collective-permute-start = (bf16[4,2,8,16,128]{4,3,2,1,0:T(8,128)(2,1)}, bf16[4,2,8,16,128]{4,3,2,1,0:T(8,128)(2,1)S(1)}, u32[]{:S(2)}, u32[]{:S(2)}) collective-permute-start(bf16[4,2,8,16,128]{4,3,2,1,0:T(8,128)(2,1)} %get-tuple-element.68), channel_id=1, source_target_pairs={{0,2},{2,0},{4,6},{6,4},{8,10},{10,8},{12,14},{14,12},{1,3},{3,1},... | collective-permute-start | bytes 786440 | tf_op jit(solution)/shard_map/ppermute | solution.py:278
  12.7 34.4 %collective-permute-start.1 = (bf16[4,2,8,16,128]{4,3,2,1,0:T(8,128)(2,1)}, bf16[4,2,8,16,128]{4,3,2,1,0:T(8,128)(2,1)S(1)}, u32[]{:S(2)}, u32[]{:S(2)}) collective-permute-start(bf16[4,2,8,16,128]{4,3,2,1,0:T(8,128)(2,1)} %get-tuple-element.72), channel_id=1, source_target_pairs={{0,4},{2,6},{4,0},{6,2},{8,12},{10,14},{12,8},{14,10},{1,5},{3,7},... | collective-permute-start | bytes 786440 | tf_op jit(solution)/shard_map/ppermute | solution.py:278
  14.3 51.4 %collective-permute-start.2 = (bf16[4,2,8,16,128]{4,3,2,1,0:T(8,128)(2,1)}, bf16[4,2,8,16,128]{4,3,2,1,0:T(8,128)(2,1)S(1)}, u32[]{:S(2)}, u32[]{:S(2)}) collective-permute-start(bf16[4,2,8,16,128]{4,3,2,1,0:T(8,128)(2,1)} %get-tuple-element.76), channel_id=1, source_target_pairs={{0,8},{2,10},{4,12},{6,14},{8,0},{10,2},{12,4},{14,6},{1,9},{3,11}... | collective-permute-start | bytes 786440 | tf_op jit(solution)/shard_map/ppermute | solution.py:278
  16.9 30.2 %collective-permute-start.4 = (bf16[4,2,8,16,128]{4,3,2,1,0:T(8,128)(2,1)}, bf16[4,2,8,16,128]{4,3,2,1,0:T(8,128)(2,1)S(1)}, u32[]{:S(2)}, u32[]{:S(2)}) collective-permute-start(bf16[4,2,8,16,128]{4,3,2,1,0:T(8,128)(2,1)} %get-tuple-element.81), channel_id=1, source_target_pairs={{0,10},{2,8},{4,14},{6,12},{8,2},{10,0},{12,6},{14,4},{1,11},{3,9}... | collective-permute-start | bytes 786440 | tf_op jit(solution)/shard_map/ppermute | solution.py:278
  17.2 49.2 %collective-permute-start.5 = (bf16[4,2,8,16,128]{4,3,2,1,0:T(8,128)(2,1)}, bf16[4,2,8,16,128]{4,3,2,1,0:T(8,128)(2,1)S(1)}, u32[]{:S(2)}, u32[]{:S(2)}) collective-permute-start(bf16[4,2,8,16,128]{4,3,2,1,0:T(8,128)(2,1)} %get-tuple-element.84), channel_id=1, source_target_pairs={{0,12},{2,14},{4,8},{6,10},{8,4},{10,6},{12,0},{14,2},{1,13},{3,15... | collective-permute-start | bytes 786440 | tf_op jit(solution)/shard_map/ppermute | solution.py:278
  47.1 69.6 %collective-permute-start.12 = (bf16[3,2,24,16,128]{4,3,2,1,0:T(8,128)(2,1)}, bf16[3,2,24,16,128]{4,3,2,1,0:T(8,128)(2,1)S(1)}, u32[]{:S(2)}, u32[]{:S(2)}) collective-permute-start(bf16[3,2,24,16,128]{4,3,2,1,0:T(8,128)(2,1)} %get-tuple-element.102), channel_id=1, source_target_pairs={{0,8},{2,10},{4,12},{6,14},{8,0},{10,2},{12,4},{14,6},{1,9},{3,11}... | collective-permute-start | bytes 1769480 | tf_op jit(solution)/shard_map/ppermute | solution.py:278
  47.1 70.6 %collective-permute-start.8 = (bf16[3,2,24,16,128]{4,3,2,1,0:T(8,128)(2,1)}, bf16[3,2,24,16,128]{4,3,2,1,0:T(8,128)(2,1)S(1)}, u32[]{:S(2)}, u32[]{:S(2)}) collective-permute-start(bf16[3,2,24,16,128]{4,3,2,1,0:T(8,128)(2,1)} %get-tuple-element.92), channel_id=1, source_target_pairs={{0,2},{2,0},{4,6},{6,4},{8,10},{10,8},{12,14},{14,12},{1,3},{3,1},... | collective-permute-start | bytes 1769480 | tf_op jit(solution)/shard_map/ppermute | solution.py:278
  48.6 35.9 %collective-permute-start.6 = (bf16[4,2,8,16,128]{4,3,2,1,0:T(8,128)(2,1)S(1)}, bf16[4,2,8,16,128]{4,3,2,1,0:T(8,128)(2,1)S(1)}, u32[]{:S(2)}, u32[]{:S(2)}) collective-permute-start(bf16[4,2,8,16,128]{4,3,2,1,0:T(8,128)(2,1)S(1)} %copy-done.4), channel_id=1, source_target_pairs={{0,14},{2,12},{4,10},{6,8},{8,6},{10,4},{12,2},{14,0},{1,15},{3,13... | collective-permute-start | bytes 786440 | tf_op jit(solution)/shard_map/ppermute | solution.py:278
  65.8 18.7 %collective-permute-start.3 = (bf16[4,2,8,16,128]{4,3,2,1,0:T(8,128)(2,1)S(1)}, bf16[4,2,8,16,128]{4,3,2,1,0:T(8,128)(2,1)S(1)}, u32[]{:S(2)}, u32[]{:S(2)}) collective-permute-start(bf16[4,2,8,16,128]{4,3,2,1,0:T(8,128)(2,1)S(1)} %copy-done.3), channel_id=1, source_target_pairs={{0,6},{2,4},{4,2},{6,0},{8,14},{10,12},{12,10},{14,8},{1,7},{3,5},... | collective-permute-start | bytes 786440 | tf_op jit(solution)/shard_map/ppermute | solution.py:278
  66.4 60.8 %collective-permute-start.14 = (bf16[3,2,24,16,128]{4,3,2,1,0:T(8,128)(2,1)}, bf16[3,2,24,16,128]{4,3,2,1,0:T(8,128)(2,1)S(1)}, u32[]{:S(2)}, u32[]{:S(2)}) collective-permute-start(bf16[3,2,24,16,128]{4,3,2,1,0:T(8,128)(2,1)} %get-tuple-element.107), channel_id=1, source_target_pairs={{0,10},{2,8},{4,14},{6,12},{8,2},{10,0},{12,6},{14,4},{1,11},{3,9}... | collective-permute-start | bytes 1769480 | tf_op jit(solution)/shard_map/ppermute | solution.py:278
  84.5 43.6 %collective-permute-start.15 = (bf16[3,2,24,16,128]{4,3,2,1,0:T(8,128)(2,1)}, bf16[3,2,24,16,128]{4,3,2,1,0:T(8,128)(2,1)S(1)}, u32[]{:S(2)}, u32[]{:S(2)}) collective-permute-start(bf16[3,2,24,16,128]{4,3,2,1,0:T(8,128)(2,1)} %get-tuple-element.110), channel_id=1, source_target_pairs={{0,12},{2,14},{4,8},{6,10},{8,4},{10,6},{12,0},{14,2},{1,13},{3,15... | collective-permute-start | bytes 1769480 | tf_op jit(solution)/shard_map/ppermute | solution.py:278
  84.5 56.1 %collective-permute-start.11 = (bf16[3,2,24,16,128]{4,3,2,1,0:T(8,128)(2,1)}, bf16[3,2,24,16,128]{4,3,2,1,0:T(8,128)(2,1)S(1)}, u32[]{:S(2)}, u32[]{:S(2)}) collective-permute-start(bf16[3,2,24,16,128]{4,3,2,1,0:T(8,128)(2,1)} %get-tuple-element.98), channel_id=1, source_target_pairs={{0,4},{2,6},{4,0},{6,2},{8,12},{10,14},{12,8},{14,10},{1,5},{3,7},... | collective-permute-start | bytes 1769480 | tf_op jit(solution)/shard_map/ppermute | solution.py:278
  116.6 46.7 %collective-permute-start.13 = (bf16[3,2,24,16,128]{4,3,2,1,0:T(8,128)(2,1)}, bf16[3,2,24,16,128]{4,3,2,1,0:T(8,128)(2,1)S(1)}, u32[]{:S(2)}, u32[]{:S(2)}) collective-permute-start(bf16[3,2,24,16,128]{4,3,2,1,0:T(8,128)(2,1)} %get-tuple-element.103), channel_id=1, source_target_pairs={{0,6},{2,4},{4,2},{6,0},{8,14},{10,12},{12,10},{14,8},{1,7},{3,5},... | collective-permute-start | bytes 1769480 | tf_op jit(solution)/shard_map/ppermute | solution.py:278
  117.7 45.7 %collective-permute-start.9 = (bf16[3,2,24,16,128]{4,3,2,1,0:T(8,128)(2,1)}, bf16[3,2,24,16,128]{4,3,2,1,0:T(8,128)(2,1)S(1)}, u32[]{:S(2)}, u32[]{:S(2)}) collective-permute-start(bf16[3,2,24,16,128]{4,3,2,1,0:T(8,128)(2,1)} %get-tuple-element.93), channel_id=1, source_target_pairs={{0,14},{2,12},{4,10},{6,8},{8,6},{10,4},{12,2},{14,0},{1,15},{3,13... | collective-permute-start | bytes 1769480 | tf_op jit(solution)/shard_map/ppermute | solution.py:278
  168.1 25.3 %collective-permute-start.16 = (bf16[8,3,2,24,16,128]{5,4,3,2,1,0:T(8,128)(2,1)}, bf16[8,3,2,24,16,128]{5,4,3,2,1,0:T(8,128)(2,1)}, u32[]{:S(2)}, u32[]{:S(2)}) collective-permute-start(bf16[8,3,2,24,16,128]{5,4,3,2,1,0:T(8,128)(2,1)} %bitcast_dynamic-update-slice_fusion.refs_2_), channel_id=1, source_target_pairs={{0,1},{1,0},{2,3},{3,2},{4,5},{5,4},{6,7},{7,6},{8,9},{9,8},{10,11... | collective-permute-start | bytes 14155784 | tf_op jit(solution)/shard_map/ppermute | solution.py:286
  168.4 25.0 %collective-permute-start.7 = (bf16[8,4,2,8,16,128]{5,4,3,2,1,0:T(8,128)(2,1)S(1)}, bf16[8,4,2,8,16,128]{5,4,3,2,1,0:T(8,128)(2,1)}, u32[]{:S(2)}, u32[]{:S(2)}) collective-permute-start(bf16[8,4,2,8,16,128]{5,4,3,2,1,0:T(8,128)(2,1)S(1)} %bitcast_dynamic-update-slice_fusion.8.refs_0_), channel_id=1, source_target_pairs={{0,1},{1,0},{2,3},{3,2},{4,5},{5,4},{6,7},{7,6},{8,9},{9,8},{10,11... | collective-permute-start | bytes 6291464 | tf_op jit(solution)/shard_map/ppermute | solution.py:286
  170.3 16.3 %collective-permute-start.17 = (bf16[1,2,24,16,128]{4,3,2,1,0:T(8,128)(2,1)S(1)}, bf16[1,2,24,16,128]{4,3,2,1,0:T(8,128)(2,1)S(1)}, u32[]{:S(2)}, u32[]{:S(2)}) collective-permute-start(bf16[1,2,24,16,128]{4,3,2,1,0:T(8,128)(2,1)S(1)} %copy-done.11), channel_id=1, source_target_pairs={{0,8},{2,10},{4,12},{6,14},{8,0},{10,2},{12,4},{14,6},{1,9},{3,11}... | collective-permute-start | bytes 589832 | tf_op jit(solution)/shard_map/ppermute | solution.py:278
  171.9 19.6 %collective-permute-start.19 = (bf16[1,2,24,16,128]{4,3,2,1,0:T(8,128)(2,1)S(1)}, bf16[1,2,24,16,128]{4,3,2,1,0:T(8,128)(2,1)S(1)}, u32[]{:S(2)}, u32[]{:S(2)}) collective-permute-start(bf16[1,2,24,16,128]{4,3,2,1,0:T(8,128)(2,1)S(1)} %copy-done.10), channel_id=1, source_target_pairs={{0,10},{2,8},{4,14},{6,12},{8,2},{10,0},{12,6},{14,4},{1,11},{3,9}... | collective-permute-start | bytes 589832 | tf_op jit(solution)/shard_map/ppermute | solution.py:278
  173.9 57.2 %collective-permute-start.10 = (bf16[1,2,24,16,128]{4,3,2,1,0:T(8,128)(2,1)S(1)}, bf16[1,2,24,16,128]{4,3,2,1,0:T(8,128)(2,1)S(1)}, u32[]{:S(2)}, u32[]{:S(2)}) collective-permute-start(bf16[1,2,24,16,128]{4,3,2,1,0:T(8,128)(2,1)S(1)} %copy-done.9), channel_id=1, source_target_pairs={{0,2},{2,0},{4,6},{6,4},{8,10},{10,8},{12,14},{14,12},{1,3},{3,1},... | collective-permute-start | bytes 589832 | tf_op jit(solution)/shard_map/ppermute | solution.py:278
  186.6 44.6 %collective-permute-start.18 = (bf16[1,2,24,16,128]{4,3,2,1,0:T(8,128)(2,1)S(1)}, bf16[1,2,24,16,128]{4,3,2,1,0:T(8,128)(2,1)S(1)}, u32[]{:S(2)}, u32[]{:S(2)}) collective-permute-start(bf16[1,2,24,16,128]{4,3,2,1,0:T(8,128)(2,1)S(1)} %copy-done.8), channel_id=1, source_target_pairs={{0,4},{2,6},{4,0},{6,2},{8,12},{10,14},{12,8},{14,10},{1,5},{3,7},... | collective-permute-start | bytes 589832 | tf_op jit(solution)/shard_map/ppermute | solution.py:278
  191.5 39.9 %collective-permute-start.21 = (bf16[1,2,24,16,128]{4,3,2,1,0:T(8,128)(2,1)S(1)}, bf16[1,2,24,16,128]{4,3,2,1,0:T(8,128)(2,1)S(1)}, u32[]{:S(2)}, u32[]{:S(2)}) collective-permute-start(bf16[1,2,24,16,128]{4,3,2,1,0:T(8,128)(2,1)S(1)} %copy-done.6), channel_id=1, source_target_pairs={{0,12},{2,14},{4,8},{6,10},{8,4},{10,6},{12,0},{14,2},{1,13},{3,15... | collective-permute-start | bytes 589832 | tf_op jit(solution)/shard_map/ppermute | solution.py:278
  193.4 37.9 %collective-permute-start.20 = (bf16[1,2,24,16,128]{4,3,2,1,0:T(8,128)(2,1)S(1)}, bf16[1,2,24,16,128]{4,3,2,1,0:T(8,128)(2,1)S(1)}, u32[]{:S(2)}, u32[]{:S(2)}) collective-permute-start(bf16[1,2,24,16,128]{4,3,2,1,0:T(8,128)(2,1)S(1)} %copy-done.7), channel_id=1, source_target_pairs={{0,6},{2,4},{4,2},{6,0},{8,14},{10,12},{12,10},{14,8},{1,7},{3,5},... | collective-permute-start | bytes 589832 | tf_op jit(solution)/shard_map/ppermute | solution.py:278
  193.4 38.0 %collective-permute-start.22 = (bf16[1,2,24,16,128]{4,3,2,1,0:T(8,128)(2,1)S(1)}, bf16[1,2,24,16,128]{4,3,2,1,0:T(8,128)(2,1)S(1)}, u32[]{:S(2)}, u32[]{:S(2)}) collective-permute-start(bf16[1,2,24,16,128]{4,3,2,1,0:T(8,128)(2,1)S(1)} %copy-done.5), channel_id=1, source_target_pairs={{0,14},{2,12},{4,10},{6,8},{8,6},{10,4},{12,2},{14,0},{1,15},{3,13... | collective-permute-start | bytes 589832 | tf_op jit(solution)/shard_map/ppermute | solution.py:278
  231.5 3.5 %collective-permute-start.23 = (bf16[8,1,2,24,16,128]{5,4,3,2,1,0:T(8,128)(2,1)S(1)}, bf16[8,1,2,24,16,128]{5,4,3,2,1,0:T(8,128)(2,1)S(1)}, u32[]{:S(2)}, u32[]{:S(2)}) collective-permute-start(bf16[8,1,2,24,16,128]{5,4,3,2,1,0:T(8,128)(2,1)S(1)} %bitcast_dynamic-update-slice_fusion.16.refs_2_), channel_id=1, source_target_pairs={{0,1},{1,0},{2,3},{3,2},{4,5},{5,4},{6,7},{7,6},{8,9},{9,8},{10,11... | collective-permute-start | bytes 4718600 | tf_op jit(solution)/shard_map/ppermute | solution.py:286
  (12 other events, 180.8 us)

commit v2 on v1

--- a/solution.py
+++ b/solution.py
@@ -42,7 +42,7 @@
 
 
 def channelize_kernel(sizes, me_ref, va_ref, vb_ref, win_ref, tab_ref, *rest):
-    feeds, chans, outs_per_dev, groups = sizes
+    feeds, chans, outs_per_dev, places = sizes
     outs, (tabs, filt) = rest[:-2], rest[-2:]
     me = me_ref[0]
     span = LANES // feeds
@@ -94,9 +94,8 @@
         product = product.reshape(2 * CH // AVG, AVG, 256)
         packed = jnp.concatenate([product[:, :, :LANES], product[:, :, LANES:]], axis=1)
         packed = packed.astype(jnp.bfloat16).reshape(chans, outs_per_dev, 2, 2 * AVG, LANES)
-        for k in range(chans):
-            for g, (first, count) in enumerate(groups):
-                outs[g * chans + k][:, :, c] = packed[k, first : first + count]
+        for out, (k, first, count) in zip(outs, places):
+            out[:, :, c] = packed[k, first : first + count]
 
 
 def channelize(voltages, me, window, table, first, steps, groups, chans):
@@ -104,18 +103,19 @@
     outs_per_dev = CH // chans // AVG
     blocks = STEP * feeds // 256
     out_shape, out_specs = [], []
-    for _, count in groups:
-        for _ in range(chans):
-            out_shape.append(
-                jax.ShapeDtypeStruct((count, 2, steps * blocks, 2 * AVG, LANES), jnp.bfloat16)
-            )
-            out_specs.append(
-                pl.BlockSpec((count, 2, blocks, 2 * AVG, LANES), lambda i, me: (0, 0, i, 0, 0))
-            )
+    places = [(k, 0, outs_per_dev) for k in range(chans // 2)]
+    places += [(k, begin, count) for begin, count in groups for k in range(chans // 2, chans)]
+    for _, _, count in places:
+        out_shape.append(
+            jax.ShapeDtypeStruct((count, 2, steps * blocks, 2 * AVG, LANES), jnp.bfloat16)
+        )
+        out_specs.append(
+            pl.BlockSpec((count, 2, blocks, 2 * AVG, LANES), lambda i, me: (0, 0, i, 0, 0))
+        )
     block = (2, feeds, STEP * CH)
     rows = steps * STEP * feeds
     result = pl.pallas_call(
-        functools.partial(channelize_kernel, (feeds, chans, outs_per_dev, groups)),
+        functools.partial(channelize_kernel, (feeds, chans, outs_per_dev, places)),
         grid_spec=pltpu.PrefetchScalarGridSpec(
             num_scalar_prefetch=1,
             grid=(steps,),
@@ -139,11 +139,17 @@
             transcendentals=0,
         ),
     )(me.reshape(1), voltages, voltages, window, table)
-    return [result[g * chans : (g + 1) * chans] for g in range(len(groups))]
+    half = chans // 2
+    near = list(result[:half])
+    far = [
+        dict(zip(range(half, chans), result[half * (g + 1) : half * (g + 2)]))
+        for g in range(len(groups))
+    ]
+    return far, near
 
 
 def correlate_kernel(sizes, feed_ref, *refs):
-    feeds, chans, pieces, norm_scale = sizes
+    feeds, chans, pieces, norm_scale, adds = sizes
     own = refs[0 : 2 * pieces : 2]
     partner = refs[1 : 2 * pieces : 2]
     select = refs[2 * pieces]
@@ -195,14 +201,20 @@
         return lax.dot_general(left, right, NT, preferred_element_type=jnp.float32)
 
     real, imag = slice(0, depth), slice(depth, 2 * depth)
-    out_ref[0, 0] = dot(rows_ref[mine, :], rows_ref[other, :]) * norm_scale
-    out_ref[1, 0] = (
+    out_re = dot(rows_ref[mine, :], rows_ref[other, :]) * norm_scale
+    out_im = (
         dot(rows_ref[mine, imag], rows_ref[other, real])
         - dot(rows_ref[mine, real], rows_ref[other, imag])
     ) * norm_scale
-
-
-def correlate(feed, pieces, select, first, count, out_count, frames, feeds, chans, result):
+    if adds:
+        before = refs[2 * pieces + 1]
+        out_re = out_re + before[0, 0]
+        out_im = out_im + before[1, 0]
+    out_ref[0, 0] = out_re
+    out_ref[1, 0] = out_im
+
+
+def correlate(feed, pieces, select, first, count, out_count, frames, feeds, chans, result, adds):
     span, total, inputs = select.shape
     half = total // 2
     operands, in_specs = [], []
@@ -222,18 +234,21 @@
     in_specs.append(
         pl.BlockSpec(select.shape, lambda o, n, feed: (0, 0, 0), pipeline_mode=pl.Buffered(1))
     )
+    out_spec = pl.BlockSpec((2, 1, half, COLS), lambda o, n, feed: (0, first + o, 0, n))
     aliases = {}
     if result is not None:
         aliases = {1 + len(operands): 0}
         operands.append(result)
-        in_specs.append(pl.BlockSpec(memory_space=pl.ANY))
+        in_specs.append(out_spec if adds else pl.BlockSpec(memory_space=pl.ANY))
     return pl.pallas_call(
-        functools.partial(correlate_kernel, (feeds, chans, len(pieces), 1.0 / (frames * AVG))),
+        functools.partial(
+            correlate_kernel, (feeds, chans, len(pieces), 1.0 / (frames * AVG), adds)
+        ),
         grid_spec=pltpu.PrefetchScalarGridSpec(
             num_scalar_prefetch=1,
             grid=(count, total // COLS),
             in_specs=in_specs,
-            out_specs=pl.BlockSpec((2, 1, half, COLS), lambda o, n, feed: (0, first + o, 0, n)),
+            out_specs=out_spec,
             scratch_shapes=[pltpu.VMEM((total, 2 * depth), jnp.bfloat16)],
         ),
         out_shape=jax.ShapeDtypeStruct((2, out_count, half, total), jnp.float32),
@@ -264,51 +279,72 @@
     ).reshape(span, 1, 2 * chans * feeds)
     select = (input_order[None, :, None] == sources).astype(jnp.bfloat16)
 
-    near, far = range(1, chans // 2), range(chans // 2, chans)
-    turns = [k for pair in zip(far, near) for k in pair] + [chans - 1]
+    near, far = list(range(1, chans // 2)), list(range(chans // 2, chans))
+    turns = [k for pair in zip(far, near) for k in pair] + far[-1:]
     flying = []
 
-    def send(blocks, order):
-        received = {}
-        for k in order:
-            block = blocks[k]
-            if len(flying) >= WINDOW:
-                store, key = flying.pop(0)
-                block, store[key] = lax.optimization_barrier((block, store[key]))
-            received[k] = lax.ppermute(block, "chan", [(c, c ^ k) for c in range(chans)])
-            flying.append((received, k))
-        return received
-
-    def share(block, received, result):
-        if result is not None:
-            received[1], result = lax.optimization_barrier((received[1], result))
-        own = jnp.stack([block] + [received[k] for k in range(1, chans)])
-        return (own, lax.ppermute(own, "feed", [(0, 1), (1, 0)])), result
+    def send(k, block, *after):
+        if len(flying) >= WINDOW:
+            store, key = flying.pop(0)
+            block, store[key] = lax.optimization_barrier((block, store[key]))
+        if after:
+            block, *after = lax.optimization_barrier((block, *after))
+        store = {k: lax.ppermute(block, "chan", [(c, c ^ k) for c in range(chans)])}
+        flying.append((store, k))
+        return store
+
+    def share(block, received, begin=0, count=None):
+        parts = [block]
+        for k in range(1, chans):
+            array = received[k][k]
+            parts.append(array if count is None or array.shape[0] == count else array[begin : begin + count])
+        own = jnp.stack(parts)
+        return own, lax.ppermute(own, "feed", [(0, 1), (1, 0)])
 
     unit = LANES // feeds
+    first = unit if steps > unit else 0
     groups = [(0, outs_per_dev)]
     if outs_per_dev > 1:
         groups = [(0, outs_per_dev - 1), (outs_per_dev - 1, 1)]
-    pieces = []
-    if steps > unit:
-        blocks = channelize(voltages, me, window, table, 0, unit, [(0, outs_per_dev)], chans)[0]
-        blocks = list(blocks)
-        pieces.append((blocks[0], send(blocks, turns)))
-        me, blocks[0] = lax.optimization_barrier((me, blocks[0]))
-        pieces[0] = (blocks[0], pieces[0][1])
-        first = unit
-    else:
-        first = 0
-    blocks = channelize(voltages, me, window, table, first, steps - first, groups, chans)
-    sent = [send(group, turns) for group in blocks[:-1]]
-    sent.append(send(blocks[-1], [*far, *near]))
-    result = None
-    shared = [share(block, received, None)[0] for block, received in pieces]
-    for group, received, (first, count) in zip(blocks, sent, groups):
-        block, result = share(group[0], received, result)
+    if first:
+        start_far, start = channelize(
+            voltages, me, window, table, 0, first, [(0, outs_per_dev)], chans
+        )
+        start_far[0].update({k: start[k] for k in near})
+        me, start[0] = lax.optimization_barrier((me, start[0]))
+    far_blocks, near_blocks = channelize(
+        voltages, me, window, table, first, steps - first, groups, chans
+    )
+    result = early = None
+    if first:
+        early = {}
+        for place, k in enumerate(turns):
+            block = start_far[0][k]
+            if place == WINDOW:
+                block, near_blocks[0] = lax.optimization_barrier((block, near_blocks[0]))
+            early[k] = send(k, block)
+    sent = [{k: None for k in near} for _ in groups]
+    for place, k in enumerate(turns):
+        block = near_blocks[k] if k in near else far_blocks[0][k]
+        if first and place == len(turns) - 2:
+            own, partner = share(start[0], early)
+            result = correlate(
+                feed, [(own, partner, 0)],
+                select, 0, outs_per_dev, outs_per_dev, frames, feeds, chans, None, False,
+            )
+            block, result = lax.optimization_barrier((block, result))
+        store = send(k, block)
+        for received in sent if k in near else sent[:1]:
+            received[k] = store
+    for k in far if len(groups) > 1 else []:
+        sent[1][k] = send(k, far_blocks[1][k])
+    for g, (begin, count) in enumerate(groups):
+        mine = near_blocks[0][begin : begin + count]
+        if g:
+            mine, result = lax.optimization_barrier((mine, result))
         result = correlate(
-            feed, [piece + (first,) for piece in shared] + [block + (0,)],
-            select, first, count, outs_per_dev, frames, feeds, chans, result,
+            feed, [share(mine, sent[g], begin, count) + (0,)],
+            select, begin, count, outs_per_dev, frames, feeds, chans, result, first > 0,
         )
     return result
 

time: 247 us -> 217 us (0.88)
  starting transfers between devices: 76.2 us -> 36.9 us
  Pallas kernels: 80.1 us -> 91 us
  local copies, waits for them, and re-layouts: 9.48 us -> 2.18 us
  waiting for transfers between devices: 79.9 us -> 83.8 us
    ppermute x24 -> x21, starting transfers between devices: 76.2 us -> 36.9 us  [the longest x18 36.7 us: send(): store = {k: lax.ppermute(block, 'chan', [(c, c ^ k) for c in range(chans)])}]
    pallas_call x2 -> x3, Pallas kernels: 47.5 us -> 58.5 us  [correlate(): pl.pallas_call(functools.partial(correlate_kernel, (feeds, chans, len(pie...]
    unnamed x45 -> x41, local copies, waits for them, and re-layouts: 8.26 us -> 1.74 us
    ppermute x24 -> x21, waiting for transfers between devices: 79.9 us -> 83.8 us  [the longest x18 80.4 us: send(): store = {k: lax.ppermute(block, 'chan', [(c, c ^ k) for c in range(chans)])}]
  transfers between devices with their start and end apart: 24 -> 21, of which waited for: 8 -> 7; matrix products, arithmetic and copies ran while one was open for 2% -> 1% of each run, Pallas kernels for 24% -> 33%
where the time goes in v2:
time: 217 us; the launch traced here: 215 us
  Pallas kernels  91 us (42%)
  waiting for transfers between devices  83.8 us (39%)
  starting transfers between devices  36.9 us (17%)
  local copies, waits for them, and re-layouts  2.18 us (1%)
    ppermute x18, waiting for transfers between devices, send(): store = {k: lax.ppermute(block, 'chan', [(c, c ^ k) for c in range(chans)])}  80.4 us
    pallas_call x3, Pallas kernels, correlate(): pl.pallas_call(functools.partial(correlate_kernel, (feeds, chans, len(pie...  58.5 us
    ppermute x18, starting transfers between devices, send(): store = {k: lax.ppermute(block, 'chan', [(c, c ^ k) for c in range(chans)])}  36.7 us
    pallas_call x2, Pallas kernels, channelize(): pl.pallas_call(functools.partial(channelize_kernel, (feeds, chans, outs_p...  32.4 us
  transfers between devices with their start and end apart: 21, of which 7 were waited for; matrix products, arithmetic and copies ran while one was open for 1% of the time, Pallas kernels for 33%

profile of v2, /device:TPU:0, one launch (start us, length us, event | category | flops | bytes accessed | tf_op | source)
XLA Modules:
  0.0 215.1 jit_solution(8293227673675181671)
XLA Ops:
  0.0 9.7 %shard_map.46 = (bf16[4,2,8,16,128]{4,3,2,1,0:T(8,128)(2,1)}, bf16[4,2,8,16,128]{4,3,2,1,0:T(8,128)(2,1)}, bf16[4,2,8,16,128]{4,3,2,1,0:T(8,128)(2,1)}, bf16[4,2...) custom-call(s32[1]{0:T(128)} %bitcast.1.me_ref, ...), custom_call_target="tpu_custom_call" | custom-call | flops 1610612736 | bytes 10485760 | tf_op jit(solution)/shard_map/pallas_call | solution.py:117
  9.7 3.1 %collective-permute-start = (bf16[4,2,8,16,128]{4,3,2,1,0:T(8,128)(2,1)}, bf16[4,2,8,16,128]{4,3,2,1,0:T(8,128)(2,1)S(1)}, u32[]{:S(2)}, u32[]{:S(2)}) collective-permute-start(bf16[4,2,8,16,128]{4,3,2,1,0:T(8,128)(2,1)} %get-tuple-element.66), channel_id=1, source_target_pairs={{0,4},{2,6},{4,0},{6,2},{8,12},{10,14},{12,8},{14,10},{1,5},{3,7},... | collective-permute-start | bytes 786440 | tf_op jit(solution)/shard_map/ppermute | solution.py:292
  12.8 2.6 %collective-permute-start.2 = (bf16[4,2,8,16,128]{4,3,2,1,0:T(8,128)(2,1)}, bf16[4,2,8,16,128]{4,3,2,1,0:T(8,128)(2,1)S(1)}, u32[]{:S(2)}, u32[]{:S(2)}) collective-permute-start(bf16[4,2,8,16,128]{4,3,2,1,0:T(8,128)(2,1)} %get-tuple-element.72), channel_id=1, source_target_pairs={{0,8},{2,10},{4,12},{6,14},{8,0},{10,2},{12,4},{14,6},{1,9},{3,11}... | collective-permute-start | bytes 786440 | tf_op jit(solution)/shard_map/ppermute | solution.py:292
  15.4 1.5 collective-permute-start.5
  17.2 2.5 %collective-permute-start.7 = (bf16[4,2,8,16,128]{4,3,2,1,0:T(8,128)(2,1)}, bf16[4,2,8,16,128]{4,3,2,1,0:T(8,128)(2,1)S(1)}, u32[]{:S(2)}, u32[]{:S(2)}) collective-permute-start(bf16[4,2,8,16,128]{4,3,2,1,0:T(8,128)(2,1)} %get-tuple-element.89), channel_id=1, source_target_pairs={{0,12},{2,14},{4,8},{6,10},{8,4},{10,6},{12,0},{14,2},{1,13},{3,15... | collective-permute-start | bytes 786440 | tf_op jit(solution)/shard_map/ppermute | solution.py:292
  19.7 22.7 %shard_map.47 = (bf16[4,2,24,16,128]{4,3,2,1,0:T(8,128)(2,1)}, bf16[4,2,24,16,128]{4,3,2,1,0:T(8,128)(2,1)}, bf16[4,2,24,16,128]{4,3,2,1,0:T(8,128)(2,1)}, bf16[...) custom-call(s32[1]{0:T(128)} %bitcast.2.me_ref, ...), custom_call_target="tpu_custom_call" | custom-call | flops 4831838208 | bytes 31457280 | tf_op jit(solution)/shard_map/pallas_call | solution.py:117
  42.5 2.4 %collective-permute-start.8 = (bf16[4,2,8,16,128]{4,3,2,1,0:T(8,128)(2,1)}, bf16[4,2,8,16,128]{4,3,2,1,0:T(8,128)(2,1)S(1)}, u32[]{:S(2)}, u32[]{:S(2)}) collective-permute-start(bf16[4,2,8,16,128]{4,3,2,1,0:T(8,128)(2,1)} %get-tuple-element.92), channel_id=1, source_target_pairs={{0,14},{2,12},{4,10},{6,8},{8,6},{10,4},{12,2},{14,0},{1,15},{3,13... | collective-permute-start | bytes 786440 | tf_op jit(solution)/shard_map/ppermute | solution.py:292
  44.9 4.9 %collective-permute-done.6 = bf16[4,2,8,16,128]{4,3,2,1,0:T(8,128)(2,1)S(1)} collective-permute-done((bf16[4,2,8,16,128]{4,3,2,1,0:T(8,128)(2,1)}, bf16[4,2,8,16,128]{4,3,2,1,0:T(8,128)(2,1)S(1)}, u32[]{:S(2)}, u32[]{:S(2)}) %collective-permute-start.6) | collective-permute-done | bytes 262176 | tf_op jit(solution)/shard_map/ppermute | solution.py:292
  49.8 4.9 %collective-permute-done.8 = bf16[4,2,8,16,128]{4,3,2,1,0:T(8,128)(2,1)S(1)} collective-permute-done((bf16[4,2,8,16,128]{4,3,2,1,0:T(8,128)(2,1)}, bf16[4,2,8,16,128]{4,3,2,1,0:T(8,128)(2,1)S(1)}, u32[]{:S(2)}, u32[]{:S(2)}) %collective-permute-start.8) | collective-permute-done | bytes 262176 | tf_op jit(solution)/shard_map/ppermute | solution.py:292
  54.7 3.1 %collective-permute-done.3 = bf16[4,2,8,16,128]{4,3,2,1,0:T(8,128)(2,1)S(1)} collective-permute-done((bf16[4,2,8,16,128]{4,3,2,1,0:T(8,128)(2,1)}, bf16[4,2,8,16,128]{4,3,2,1,0:T(8,128)(2,1)S(1)}, u32[]{:S(2)}, u32[]{:S(2)}) %collective-permute-start.3) | collective-permute-done | bytes 262176 | tf_op jit(solution)/shard_map/ppermute | solution.py:292
  58.1 6.2 %collective-permute-start.10 = (bf16[3,2,24,16,128]{4,3,2,1,0:T(8,128)(2,1)}, bf16[3,2,24,16,128]{4,3,2,1,0:T(8,128)(2,1)S(1)}, u32[]{:S(2)}, u32[]{:S(2)}) collective-permute-start(bf16[3,2,24,16,128]{4,3,2,1,0:T(8,128)(2,1)} %get-tuple-element.95), channel_id=1, source_target_pairs={{0,8},{2,10},{4,12},{6,14},{8,0},{10,2},{12,4},{14,6},{1,9},{3,11}... | collective-permute-start | bytes 1769480 | tf_op jit(solution)/shard_map/ppermute | solution.py:292
  64.7 1.5 collective-permute-start.1
  66.2 1.3 collective-permute-start.13
  67.5 2.1 collective-permute-start.4
  70.4 19.9 %shard_map.48.refs_3_ = f32[2,4,512,1024]{3,2,1,0:T(8,128)} custom-call(s32[1]{0:T(128)} %bitcast.feed_ref, bf16[8,4,2,8,16,128]{5,4,3,2,1,0:T(8,128)(2,1)S(1)} %bitcast_dynamic-update-slice_fusion.8.refs_0_, bf16[8,4,2,8,16,128]{5,4,3,2,1,0:T(8,128)(2,1)} %collective-permute-done.9.refs_1_, bf16[2,1024,1024]{2,1,0:T(8,128)(2,1)S(1)} %compare_convert_fusion.refs_2_), custom_call_target="tpu_custom_call" | custom-call | flops 1000 | bytes 1000 | tf_op jit(solution)/shard_map/pallas_call | solution.py:243
  90.3 26.4 %collective-permute-done.10 = bf16[3,2,24,16,128]{4,3,2,1,0:T(8,128)(2,1)S(1)} collective-permute-done((bf16[3,2,24,16,128]{4,3,2,1,0:T(8,128)(2,1)}, bf16[3,2,24,16,128]{4,3,2,1,0:T(8,128)(2,1)S(1)}, u32[]{:S(2)}, u32[]{:S(2)}) %collective-permute-start.10) | collective-permute-done | bytes 589856 | tf_op jit(solution)/shard_map/ppermute | solution.py:292
  116.8 13.5 %collective-permute-done.12 = bf16[3,2,24,16,128]{4,3,2,1,0:T(8,128)(2,1)S(1)} collective-permute-done((bf16[3,2,24,16,128]{4,3,2,1,0:T(8,128)(2,1)}, bf16[3,2,24,16,128]{4,3,2,1,0:T(8,128)(2,1)S(1)}, u32[]{:S(2)}, u32[]{:S(2)}) %collective-permute-start.12) | collective-permute-done | bytes 589856 | tf_op jit(solution)/shard_map/ppermute | solution.py:292
  131.9 27.6 %collective-permute-done.11 = bf16[4,2,24,16,128]{4,3,2,1,0:T(8,128)(2,1)S(1)} collective-permute-done((bf16[4,2,24,16,128]{4,3,2,1,0:T(8,128)(2,1)S(1)}, bf16[4,2,24,16,128]{4,3,2,1,0:T(8,128)(2,1)S(1)}, u32[]{:S(2)}, u32[]{:S(2)}) %collective-permute-start.11) | collective-permute-done | bytes 786464 | tf_op jit(solution)/shard_map/ppermute | solution.py:292
  160.7 7.9 %collective-permute-start.16 = (bf16[1,2,24,16,128]{4,3,2,1,0:T(8,128)(2,1)S(1)}, bf16[1,2,24,16,128]{4,3,2,1,0:T(8,128)(2,1)S(1)}, u32[]{:S(2)}, u32[]{:S(2)}) collective-permute-start(bf16[1,2,24,16,128]{4,3,2,1,0:T(8,128)(2,1)S(1)} %copy-done.9), channel_id=1, source_target_pairs={{0,8},{2,10},{4,12},{6,14},{8,0},{10,2},{12,4},{14,6},{1,9},{3,11}... | collective-permute-start | bytes 589832 | tf_op jit(solution)/shard_map/ppermute | solution.py:292
  168.7 2.5 %collective-permute-start.18 = (bf16[1,2,24,16,128]{4,3,2,1,0:T(8,128)(2,1)S(1)}, bf16[1,2,24,16,128]{4,3,2,1,0:T(8,128)(2,1)S(1)}, u32[]{:S(2)}, u32[]{:S(2)}) collective-permute-start(bf16[1,2,24,16,128]{4,3,2,1,0:T(8,128)(2,1)S(1)} %copy-done.7), channel_id=1, source_target_pairs={{0,12},{2,14},{4,8},{6,10},{8,4},{10,6},{12,0},{14,2},{1,13},{3,15... | collective-permute-start | bytes 589832 | tf_op jit(solution)/shard_map/ppermute | solution.py:292
  171.2 1.4 collective-permute-start.19
  172.6 28.2 %shard_map.49.refs_3_ = f32[2,4,512,1024]{3,2,1,0:T(8,128)} custom-call(s32[1]{0:T(128)} %bitcast.feed_ref, bf16[8,3,2,24,16,128]{5,4,3,2,1,0:T(8,128)(2,1)S(1)} %bitcast_dynamic-update-slice_fusion.refs_0_, bf16[8,3,2,24,16,128]{5,4,3,2,1,0:T(8,128)(2,1)S(1)} %collective-permute-done.15.refs_1_, ...), custom_call_target="tpu_custom_call", output_to_operand_aliasing={{}: (4, {})} | custom-call | flops 1000 | bytes 1000 | tf_op jit(solution)/shard_map/pallas_call | solution.py:243
  201.2 3.4 %collective-permute-done.20.refs_1_ = bf16[8,1,2,24,16,128]{5,4,3,2,1,0:T(8,128)(2,1)S(1)} collective-permute-done((bf16[8,1,2,24,16,128]{5,4,3,2,1,0:T(8,128)(2,1)S(1)}, bf16[8,1,2,24,16,128]{5,4,3,2,1,0:T(8,128)(2,1)S(1)}, u32[]{:S(2)}, u32[]{:S(2)}) %collective-permute-start.20) | collective-permute-done | bytes 1572896 | tf_op jit(solution)/shard_map/ppermute | solution.py:302
  204.6 10.5 %shard_map.50 = f32[2,4,512,1024]{3,2,1,0:T(8,128)} custom-call(s32[1]{0:T(128)} %bitcast.feed_ref, bf16[8,1,2,24,16,128]{5,4,3,2,1,0:T(8,128)(2,1)S(1)} %bitcast_dynamic-update-slice_fusion.16.refs_0_, bf16[8,1,2,24,16,128]{5,4,3,2,1,0:T(8,128)(2,1)S(1)} %collective-permute-done.20.refs_1_, ...), custom_call_target="tpu_custom_call", output_to_operand_aliasing={{}: (4, {})} | custom-call | flops 1000 | bytes 1000 | tf_op jit(solution)/shard_map/pallas_call | solution.py:243
  (78 shorter events, 4.9 us)
Async XLA Ops:
  9.7 35.2 %collective-permute-start = (bf16[4,2,8,16,128]{4,3,2,1,0:T(8,128)(2,1)}, bf16[4,2,8,16,128]{4,3,2,1,0:T(8,128)(2,1)S(1)}, u32[]{:S(2)}, u32[]{:S(2)}) collective-permute-start(bf16[4,2,8,16,128]{4,3,2,1,0:T(8,128)(2,1)} %get-tuple-element.66), channel_id=1, source_target_pairs={{0,4},{2,6},{4,0},{6,2},{8,12},{10,14},{12,8},{14,10},{1,5},{3,7},... | collective-permute-start | bytes 786440 | tf_op jit(solution)/shard_map/ppermute | solution.py:292
  12.8 32.0 %collective-permute-start.2 = (bf16[4,2,8,16,128]{4,3,2,1,0:T(8,128)(2,1)}, bf16[4,2,8,16,128]{4,3,2,1,0:T(8,128)(2,1)S(1)}, u32[]{:S(2)}, u32[]{:S(2)}) collective-permute-start(bf16[4,2,8,16,128]{4,3,2,1,0:T(8,128)(2,1)} %get-tuple-element.72), channel_id=1, source_target_pairs={{0,8},{2,10},{4,12},{6,14},{8,0},{10,2},{12,4},{14,6},{1,9},{3,11}... | collective-permute-start | bytes 786440 | tf_op jit(solution)/shard_map/ppermute | solution.py:292
  15.4 27.1 %collective-permute-start.5 = (bf16[4,2,8,16,128]{4,3,2,1,0:T(8,128)(2,1)}, bf16[4,2,8,16,128]{4,3,2,1,0:T(8,128)(2,1)S(1)}, u32[]{:S(2)}, u32[]{:S(2)}) collective-permute-start(bf16[4,2,8,16,128]{4,3,2,1,0:T(8,128)(2,1)} %get-tuple-element.80), channel_id=1, source_target_pairs={{0,2},{2,0},{4,6},{6,4},{8,10},{10,8},{12,14},{14,12},{1,3},{3,1},... | collective-permute-start | bytes 786440 | tf_op jit(solution)/shard_map/ppermute | solution.py:292
  16.9 32.9 %collective-permute-start.6 = (bf16[4,2,8,16,128]{4,3,2,1,0:T(8,128)(2,1)}, bf16[4,2,8,16,128]{4,3,2,1,0:T(8,128)(2,1)S(1)}, u32[]{:S(2)}, u32[]{:S(2)}) collective-permute-start(bf16[4,2,8,16,128]{4,3,2,1,0:T(8,128)(2,1)} %get-tuple-element.86), channel_id=1, source_target_pairs={{0,10},{2,8},{4,14},{6,12},{8,2},{10,0},{12,6},{14,4},{1,11},{3,9}... | collective-permute-start | bytes 786440 | tf_op jit(solution)/shard_map/ppermute | solution.py:292
  17.2 32.6 %collective-permute-start.7 = (bf16[4,2,8,16,128]{4,3,2,1,0:T(8,128)(2,1)}, bf16[4,2,8,16,128]{4,3,2,1,0:T(8,128)(2,1)S(1)}, u32[]{:S(2)}, u32[]{:S(2)}) collective-permute-start(bf16[4,2,8,16,128]{4,3,2,1,0:T(8,128)(2,1)} %get-tuple-element.89), channel_id=1, source_target_pairs={{0,12},{2,14},{4,8},{6,10},{8,4},{10,6},{12,0},{14,2},{1,13},{3,15... | collective-permute-start | bytes 786440 | tf_op jit(solution)/shard_map/ppermute | solution.py:292
  42.5 12.3 %collective-permute-start.8 = (bf16[4,2,8,16,128]{4,3,2,1,0:T(8,128)(2,1)}, bf16[4,2,8,16,128]{4,3,2,1,0:T(8,128)(2,1)S(1)}, u32[]{:S(2)}, u32[]{:S(2)}) collective-permute-start(bf16[4,2,8,16,128]{4,3,2,1,0:T(8,128)(2,1)} %get-tuple-element.92), channel_id=1, source_target_pairs={{0,14},{2,12},{4,10},{6,8},{8,6},{10,4},{12,2},{14,0},{1,15},{3,13... | collective-permute-start | bytes 786440 | tf_op jit(solution)/shard_map/ppermute | solution.py:292
  44.8 13.0 %collective-permute-start.3 = (bf16[4,2,8,16,128]{4,3,2,1,0:T(8,128)(2,1)}, bf16[4,2,8,16,128]{4,3,2,1,0:T(8,128)(2,1)S(1)}, u32[]{:S(2)}, u32[]{:S(2)}) collective-permute-start(bf16[4,2,8,16,128]{4,3,2,1,0:T(8,128)(2,1)} %get-tuple-element.73), channel_id=1, source_target_pairs={{0,6},{2,4},{4,2},{6,0},{8,14},{10,12},{12,10},{14,8},{1,7},{3,5},... | collective-permute-start | bytes 786440 | tf_op jit(solution)/shard_map/ppermute | solution.py:292
  58.0 9.5 %collective-permute-start.9 = (bf16[8,4,2,8,16,128]{5,4,3,2,1,0:T(8,128)(2,1)S(1)}, bf16[8,4,2,8,16,128]{5,4,3,2,1,0:T(8,128)(2,1)}, u32[]{:S(2)}, u32[]{:S(2)}) collective-permute-start(bf16[8,4,2,8,16,128]{5,4,3,2,1,0:T(8,128)(2,1)S(1)} %bitcast_dynamic-update-slice_fusion.8.refs_0_), channel_id=1, source_target_pairs={{0,1},{1,0},{2,3},{3,2},{4,5},{5,4},{6,7},{7,6},{8,9},{9,8},{10,11... | collective-permute-start | bytes 6291464 | tf_op jit(solution)/shard_map/ppermute | solution.py:302
  58.1 58.5 %collective-permute-start.10 = (bf16[3,2,24,16,128]{4,3,2,1,0:T(8,128)(2,1)}, bf16[3,2,24,16,128]{4,3,2,1,0:T(8,128)(2,1)S(1)}, u32[]{:S(2)}, u32[]{:S(2)}) collective-permute-start(bf16[3,2,24,16,128]{4,3,2,1,0:T(8,128)(2,1)} %get-tuple-element.95), channel_id=1, source_target_pairs={{0,8},{2,10},{4,12},{6,14},{8,0},{10,2},{12,4},{14,6},{1,9},{3,11}... | collective-permute-start | bytes 1769480 | tf_op jit(solution)/shard_map/ppermute | solution.py:292
  64.7 65.6 %collective-permute-start.1 = (bf16[4,2,24,16,128]{4,3,2,1,0:T(8,128)(2,1)}, bf16[4,2,24,16,128]{4,3,2,1,0:T(8,128)(2,1)S(1)}, u32[]{:S(2)}, u32[]{:S(2)}) collective-permute-start(bf16[4,2,24,16,128]{4,3,2,1,0:T(8,128)(2,1)} %get-tuple-element.67), channel_id=1, source_target_pairs={{0,2},{2,0},{4,6},{6,4},{8,10},{10,8},{12,14},{14,12},{1,3},{3,1},... | collective-permute-start | bytes 2359304 | tf_op jit(solution)/shard_map/ppermute | solution.py:292
  66.2 64.1 %collective-permute-start.12 = (bf16[3,2,24,16,128]{4,3,2,1,0:T(8,128)(2,1)}, bf16[3,2,24,16,128]{4,3,2,1,0:T(8,128)(2,1)S(1)}, u32[]{:S(2)}, u32[]{:S(2)}) collective-permute-start(bf16[3,2,24,16,128]{4,3,2,1,0:T(8,128)(2,1)} %get-tuple-element.100), channel_id=1, source_target_pairs={{0,10},{2,8},{4,14},{6,12},{8,2},{10,0},{12,6},{14,4},{1,11},{3,9}... | collective-permute-start | bytes 1769480 | tf_op jit(solution)/shard_map/ppermute | solution.py:292
  66.2 65.6 %collective-permute-start.13 = (bf16[3,2,24,16,128]{4,3,2,1,0:T(8,128)(2,1)}, bf16[3,2,24,16,128]{4,3,2,1,0:T(8,128)(2,1)S(1)}, u32[]{:S(2)}, u32[]{:S(2)}) collective-permute-start(bf16[3,2,24,16,128]{4,3,2,1,0:T(8,128)(2,1)} %get-tuple-element.103), channel_id=1, source_target_pairs={{0,12},{2,14},{4,8},{6,10},{8,4},{10,6},{12,0},{14,2},{1,13},{3,15... | collective-permute-start | bytes 1769480 | tf_op jit(solution)/shard_map/ppermute | solution.py:292
  67.5 64.2 %collective-permute-start.4 = (bf16[4,2,24,16,128]{4,3,2,1,0:T(8,128)(2,1)S(1)}, bf16[4,2,24,16,128]{4,3,2,1,0:T(8,128)(2,1)S(1)}, u32[]{:S(2)}, u32[]{:S(2)}) collective-permute-start(bf16[4,2,24,16,128]{4,3,2,1,0:T(8,128)(2,1)S(1)} %copy-done.4), channel_id=1, source_target_pairs={{0,4},{2,6},{4,0},{6,2},{8,12},{10,14},{12,8},{14,10},{1,5},{3,7},... | collective-permute-start | bytes 2359304 | tf_op jit(solution)/shard_map/ppermute | solution.py:292
  70.4 46.3 %copy-start.3 = (bf16[4,2,24,16,128]{4,3,2,1,0:T(8,128)(2,1)S(1)}, bf16[4,2,24,16,128]{4,3,2,1,0:T(8,128)(2,1)}, u32[]{:S(2)}) copy-start(bf16[4,2,24,16,128]{4,3,2,1,0:T(8,128)(2,1)} %get-tuple-element.96) | copy-start | bytes 2359300
  70.4 46.3 %copy-start = (bf16[4,2,24,16,128]{4,3,2,1,0:T(8,128)(2,1)S(1)}, bf16[4,2,24,16,128]{4,3,2,1,0:T(8,128)(2,1)}, u32[]{:S(2)}) copy-start(bf16[4,2,24,16,128]{4,3,2,1,0:T(8,128)(2,1)} %get-tuple-element.63) | copy-start | bytes 2359300
  70.4 59.9 %copy-start.5 = (bf16[3,2,24,16,128]{4,3,2,1,0:T(8,128)(2,1)S(1)}, bf16[3,2,24,16,128]{4,3,2,1,0:T(8,128)(2,1)}, u32[]{:S(2)}) copy-start(bf16[3,2,24,16,128]{4,3,2,1,0:T(8,128)(2,1)} %get-tuple-element.105) | copy-start | bytes 1769476
  116.7 42.8 %collective-permute-start.11 = (bf16[4,2,24,16,128]{4,3,2,1,0:T(8,128)(2,1)S(1)}, bf16[4,2,24,16,128]{4,3,2,1,0:T(8,128)(2,1)S(1)}, u32[]{:S(2)}, u32[]{:S(2)}) collective-permute-start(bf16[4,2,24,16,128]{4,3,2,1,0:T(8,128)(2,1)S(1)} %copy-done.3), channel_id=1, source_target_pairs={{0,6},{2,4},{4,2},{6,0},{8,14},{10,12},{12,10},{14,8},{1,7},{3,5},... | collective-permute-start | bytes 2359304 | tf_op jit(solution)/shard_map/ppermute | solution.py:292
  130.3 29.9 %collective-permute-start.14 = (bf16[3,2,24,16,128]{4,3,2,1,0:T(8,128)(2,1)S(1)}, bf16[3,2,24,16,128]{4,3,2,1,0:T(8,128)(2,1)S(1)}, u32[]{:S(2)}, u32[]{:S(2)}) collective-permute-start(bf16[3,2,24,16,128]{4,3,2,1,0:T(8,128)(2,1)S(1)} %copy-done.5), channel_id=1, source_target_pairs={{0,14},{2,12},{4,10},{6,8},{8,6},{10,4},{12,2},{14,0},{1,15},{3,13... | collective-permute-start | bytes 1769480 | tf_op jit(solution)/shard_map/ppermute | solution.py:292
  160.3 12.3 %collective-permute-start.15 = (bf16[8,3,2,24,16,128]{5,4,3,2,1,0:T(8,128)(2,1)S(1)}, bf16[8,3,2,24,16,128]{5,4,3,2,1,0:T(8,128)(2,1)S(1)}, u32[]{:S(2)}, u32[]{:S(2)}) collective-permute-start(bf16[8,3,2,24,16,128]{5,4,3,2,1,0:T(8,128)(2,1)S(1)} %bitcast_dynamic-update-slice_fusion.refs_0_), channel_id=1, source_target_pairs={{0,1},{1,0},{2,3},{3,2},{4,5},{5,4},{6,7},{7,6},{8,9},{9,8},{10,11... | collective-permute-start | bytes 14155784 | tf_op jit(solution)/shard_map/ppermute | solution.py:302
  160.7 40.2 %collective-permute-start.16 = (bf16[1,2,24,16,128]{4,3,2,1,0:T(8,128)(2,1)S(1)}, bf16[1,2,24,16,128]{4,3,2,1,0:T(8,128)(2,1)S(1)}, u32[]{:S(2)}, u32[]{:S(2)}) collective-permute-start(bf16[1,2,24,16,128]{4,3,2,1,0:T(8,128)(2,1)S(1)} %copy-done.9), channel_id=1, source_target_pairs={{0,8},{2,10},{4,12},{6,14},{8,0},{10,2},{12,4},{14,6},{1,9},{3,11}... | collective-permute-start | bytes 589832 | tf_op jit(solution)/shard_map/ppermute | solution.py:292
  168.7 32.3 %collective-permute-start.18 = (bf16[1,2,24,16,128]{4,3,2,1,0:T(8,128)(2,1)S(1)}, bf16[1,2,24,16,128]{4,3,2,1,0:T(8,128)(2,1)S(1)}, u32[]{:S(2)}, u32[]{:S(2)}) collective-permute-start(bf16[1,2,24,16,128]{4,3,2,1,0:T(8,128)(2,1)S(1)} %copy-done.7), channel_id=1, source_target_pairs={{0,12},{2,14},{4,8},{6,10},{8,4},{10,6},{12,0},{14,2},{1,13},{3,15... | collective-permute-start | bytes 589832 | tf_op jit(solution)/shard_map/ppermute | solution.py:292
  171.2 29.7 %collective-permute-start.17 = (bf16[1,2,24,16,128]{4,3,2,1,0:T(8,128)(2,1)S(1)}, bf16[1,2,24,16,128]{4,3,2,1,0:T(8,128)(2,1)S(1)}, u32[]{:S(2)}, u32[]{:S(2)}) collective-permute-start(bf16[1,2,24,16,128]{4,3,2,1,0:T(8,128)(2,1)S(1)} %copy-done.8), channel_id=1, source_target_pairs={{0,10},{2,8},{4,14},{6,12},{8,2},{10,0},{12,6},{14,4},{1,11},{3,9}... | collective-permute-start | bytes 589832 | tf_op jit(solution)/shard_map/ppermute | solution.py:292
  171.2 29.8 %collective-permute-start.19 = (bf16[1,2,24,16,128]{4,3,2,1,0:T(8,128)(2,1)S(1)}, bf16[1,2,24,16,128]{4,3,2,1,0:T(8,128)(2,1)S(1)}, u32[]{:S(2)}, u32[]{:S(2)}) collective-permute-start(bf16[1,2,24,16,128]{4,3,2,1,0:T(8,128)(2,1)S(1)} %copy-done.6), channel_id=1, source_target_pairs={{0,14},{2,12},{4,10},{6,8},{8,6},{10,4},{12,2},{14,0},{1,15},{3,13... | collective-permute-start | bytes 589832 | tf_op jit(solution)/shard_map/ppermute | solution.py:292
  201.1 3.5 %collective-permute-start.20 = (bf16[8,1,2,24,16,128]{5,4,3,2,1,0:T(8,128)(2,1)S(1)}, bf16[8,1,2,24,16,128]{5,4,3,2,1,0:T(8,128)(2,1)S(1)}, u32[]{:S(2)}, u32[]{:S(2)}) collective-permute-start(bf16[8,1,2,24,16,128]{5,4,3,2,1,0:T(8,128)(2,1)S(1)} %bitcast_dynamic-update-slice_fusion.16.refs_0_), channel_id=1, source_target_pairs={{0,1},{1,0},{2,3},{3,2},{4,5},{5,4},{6,7},{7,6},{8,9},{9,8},{10,11... | collective-permute-start | bytes 4718600 | tf_op jit(solution)/shard_map/ppermute | solution.py:302
  (7 other events, 105.2 us)

commit v3 on v2

--- a/solution.py
+++ b/solution.py
@@ -14,7 +14,7 @@
 AVG = 8
 LANES = 128
 STEP = 16
-COLS = 256
+COLS = 512
 VMEM = 60 * 1024 * 1024
 WINDOW = 5
 NT = (((1,), (1,)), ((), ()))
@@ -149,48 +149,60 @@
 
 
 def correlate_kernel(sizes, feed_ref, *refs):
-    feeds, chans, pieces, norm_scale, adds = sizes
-    own = refs[0 : 2 * pieces : 2]
-    partner = refs[1 : 2 * pieces : 2]
+    feeds, pieces, norm_scale, adds, copies, begin = sizes
+    own = [(ref, k) for ref in refs[0 : 2 * pieces : 2] for k in range(ref.shape[0])]
+    partner = [(ref, k) for ref in refs[1 : 2 * pieces : 2] for k in range(ref.shape[0])]
     select = refs[2 * pieces]
-    out_ref, rows_ref = refs[-2:]
+    if copies:
+        out_ref, rows_ref, before_ref, sem = refs[-4:]
+        before = pltpu.make_async_copy(
+            refs[2 * pieces + 1].at[:, begin + pl.program_id(0)], before_ref, sem
+        )
+    else:
+        out_ref, rows_ref = refs[-2:]
     span = LANES // feeds
-    inputs = select.shape[1]
     depth = rows_ref.shape[1] // 2
+    lines = depth // span
 
     @pl.when(pl.program_id(1) == 0)
     def _():
-        low = lax.broadcasted_iota(jnp.int32, (256, LANES), 1) // feeds
-        base = 0
-        for piece in range(pieces):
-            lines = own[piece].shape[3] * 16
-            for x in range(span):
-                for first in range(0, 2 * lines, 256):
-                    tiles = []
-                    for ref in (own[piece], partner[piece]):
-                        for j in range(chans // span):
-                            tile = None
-                            for slot in range(span):
-                                source = ref[j * span + (slot ^ x), 0].reshape(2 * lines, LANES)
-                                source = source[first : first + 256]
-                                tile = source if tile is None else jnp.where(low == slot, source, tile)
-                            tiles.append(tile)
-                    value = lax.dot_general(
-                        select[x],
-                        jnp.concatenate(tiles, axis=1),
-                        NT,
-                        preferred_element_type=jnp.float32,
-                    ).astype(jnp.bfloat16)
-                    start = first
-                    while start < first + 256:
-                        q, line = start // lines, start % lines
-                        count = min(lines - line, first + 256 - start)
-                        place = q * depth + base + line
-                        rows_ref[:, place : place + count] = value[
-                            :, start - first : start - first + count
-                        ]
-                        start += count
-                base += lines
+        if copies:
+            before.start()
+        lane_slot = lax.broadcasted_iota(jnp.int32, (256, LANES), 1) // feeds
+        for x in range(span):
+            for first in range(0, 2 * lines, 256):
+                tiles = []
+                for blocks in (own, partner):
+                    for j in range(0, len(blocks), span):
+                        tile = None
+                        for slot in range(span):
+                            ref, k = blocks[j + (slot ^ x)]
+                            source = ref[k, 0].reshape(2 * lines, LANES)[first : first + 256]
+                            if tile is None:
+                                tile = source
+                            else:
+                                tile = jnp.where(lane_slot == slot, source, tile)
+                        for bit in (1 << n for n in range(x.bit_length()) if x >> n & 1):
+                            shift = bit * feeds
+                            left = pltpu.roll(tile, LANES - shift, 1)
+                            right = pltpu.roll(tile, shift, 1)
+                            tile = jnp.where((lane_slot & bit) == 0, left, right)
+                        tiles.append(tile)
+                value = lax.dot_general(
+                    select[...], jnp.concatenate(tiles, axis=1), NT, preferred_element_type=jnp.float32
+                ).astype(jnp.bfloat16)
+                start = first
+                while start < first + 256:
+                    q, line = start // lines, start % lines
+                    count = min(lines - line, first + 256 - start)
+                    place = q * depth + x * lines + line
+                    rows_ref[:, place : place + count] = value[
+                        :, start - first : start - first + count
+                    ]
+                    start += count
+
+        if copies:
+            before.wait()
 
     half = out_ref.shape[2]
     mine = pl.ds(pl.multiple_of(feed_ref[0] * half, half), half)
@@ -206,50 +218,54 @@
         dot(rows_ref[mine, imag], rows_ref[other, real])
         - dot(rows_ref[mine, real], rows_ref[other, imag])
     ) * norm_scale
-    if adds:
-        before = refs[2 * pieces + 1]
-        out_re = out_re + before[0, 0]
-        out_im = out_im + before[1, 0]
+    if copies:
+        out_re = out_re + before_ref[0, :, other]
+        out_im = out_im + before_ref[1, :, other]
+    elif adds:
+        out_re = out_re + refs[2 * pieces + 1][0, 0]
+        out_im = out_im + refs[2 * pieces + 1][1, 0]
     out_ref[0, 0] = out_re
     out_ref[1, 0] = out_im
 
 
-def correlate(feed, pieces, select, first, count, out_count, frames, feeds, chans, result, adds):
-    span, total, inputs = select.shape
+def correlate(feed, pieces, select, first, count, out_count, frames, feeds, result, adds):
+    span = LANES // feeds
+    total = select.shape[0]
     half = total // 2
     operands, in_specs = [], []
-    depth = 0
-    for own, partner, place in pieces:
-        block = (chans, 1) + own.shape[2:]
-        for array in (own, partner):
+    for pair in pieces:
+        for array in pair:
             operands.append(array)
             in_specs.append(
                 pl.BlockSpec(
-                    block,
-                    functools.partial(lambda place, o, n, feed: (0, place + o, 0, 0, 0, 0), place),
+                    (array.shape[0], 1) + array.shape[2:], lambda o, n, feed: (0, o, 0, 0, 0, 0)
                 )
             )
-        depth += own.shape[3] * 16 * span
+    depth = array.shape[3] * 16 * span
     operands.append(select)
     in_specs.append(
-        pl.BlockSpec(select.shape, lambda o, n, feed: (0, 0, 0), pipeline_mode=pl.Buffered(1))
+        pl.BlockSpec(select.shape, lambda o, n, feed: (0, 0), pipeline_mode=pl.Buffered(1))
     )
     out_spec = pl.BlockSpec((2, 1, half, COLS), lambda o, n, feed: (0, first + o, 0, n))
+    copies = adds and count == 1
     aliases = {}
     if result is not None:
         aliases = {1 + len(operands): 0}
         operands.append(result)
-        in_specs.append(out_spec if adds else pl.BlockSpec(memory_space=pl.ANY))
+        in_specs.append(out_spec if adds and not copies else pl.BlockSpec(memory_space=pl.ANY))
+    scratch = [pltpu.VMEM((total, 2 * depth), jnp.bfloat16)]
+    if copies:
+        scratch += [pltpu.VMEM((2, half, total), jnp.float32), pltpu.SemaphoreType.DMA]
     return pl.pallas_call(
         functools.partial(
-            correlate_kernel, (feeds, chans, len(pieces), 1.0 / (frames * AVG), adds)
+            correlate_kernel, (feeds, len(pieces), 1.0 / (frames * AVG), adds, copies, first)
         ),
         grid_spec=pltpu.PrefetchScalarGridSpec(
             num_scalar_prefetch=1,
             grid=(count, total // COLS),
             in_specs=in_specs,
             out_specs=out_spec,
-            scratch_shapes=[pltpu.VMEM((total, 2 * depth), jnp.bfloat16)],
+            scratch_shapes=scratch,
         ),
         out_shape=jax.ShapeDtypeStruct((2, out_count, half, total), jnp.float32),
         input_output_aliases=aliases,
@@ -266,18 +282,15 @@
     frames = voltages.shape[2] // CH - TAPS + 1
     steps = frames // STEP
     outs_per_dev = CH // chans // AVG
-    span = LANES // feeds
     window = jnp.asarray(make_window())
     table = jnp.asarray(make_table())
 
-    k = jnp.arange(chans, dtype=jnp.int32)
-    k = (k[None, :] // span) * span + ((k[None, :] % span) ^ jnp.arange(span, dtype=jnp.int32)[:, None])
     sources = (
-        ((feed ^ jnp.arange(2, dtype=jnp.int32)) * (chans * feeds))[None, :, None, None]
-        + ((me ^ k) * feeds)[:, None, :, None]
-        + jnp.arange(feeds, dtype=jnp.int32)[None, None, None, :]
-    ).reshape(span, 1, 2 * chans * feeds)
-    select = (input_order[None, :, None] == sources).astype(jnp.bfloat16)
+        ((feed ^ jnp.arange(2, dtype=jnp.int32)) * (chans * feeds))[:, None, None]
+        + ((me ^ jnp.arange(chans, dtype=jnp.int32)) * feeds)[None, :, None]
+        + jnp.arange(feeds, dtype=jnp.int32)[None, None, :]
+    ).reshape(1, 2 * chans * feeds)
+    select = (input_order[:, None] == sources).astype(jnp.bfloat16)
 
     near, far = list(range(1, chans // 2)), list(range(chans // 2, chans))
     turns = [k for pair in zip(far, near) for k in pair] + far[-1:]
@@ -293,13 +306,17 @@
         flying.append((store, k))
         return store
 
-    def share(block, received, begin=0, count=None):
+    def share(block, received, cuts, begin=0, count=None):
         parts = [block]
         for k in range(1, chans):
             array = received[k][k]
-            parts.append(array if count is None or array.shape[0] == count else array[begin : begin + count])
-        own = jnp.stack(parts)
-        return own, lax.ppermute(own, "feed", [(0, 1), (1, 0)])
+            whole = count is None or array.shape[0] == count
+            parts.append(array if whole else array[begin : begin + count])
+        pieces = []
+        for low, high in zip([0] + cuts, cuts):
+            own = jnp.stack(parts[low:high])
+            pieces.append((own, lax.ppermute(own, "feed", [(0, 1), (1, 0)])))
+        return pieces
 
     unit = LANES // feeds
     first = unit if steps > unit else 0
@@ -327,10 +344,9 @@
     for place, k in enumerate(turns):
         block = near_blocks[k] if k in near else far_blocks[0][k]
         if first and place == len(turns) - 2:
-            own, partner = share(start[0], early)
             result = correlate(
-                feed, [(own, partner, 0)],
-                select, 0, outs_per_dev, outs_per_dev, frames, feeds, chans, None, False,
+                feed, share(start[0], early, [chans]),
+                select, 0, outs_per_dev, outs_per_dev, frames, feeds, None, False,
             )
             block, result = lax.optimization_barrier((block, result))
         store = send(k, block)
@@ -343,8 +359,8 @@
         if g:
             mine, result = lax.optimization_barrier((mine, result))
         result = correlate(
-            feed, [share(mine, sent[g], begin, count) + (0,)],
-            select, begin, count, outs_per_dev, frames, feeds, chans, result, first > 0,
+            feed, share(mine, sent[g], [chans], begin, count),
+            select, begin, count, outs_per_dev, frames, feeds, result, first > 0,
         )
     return result
 

time: 217 us -> 214 us (0.986)
  Pallas kernels: 91 us -> 82.9 us
  waiting for transfers between devices: 83.8 us -> 89.1 us
    pallas_call x3, Pallas kernels: 58.5 us -> 50.3 us  [correlate(): pl.pallas_call(functools.partial(correlate_kernel, (feeds, len(pieces), 1...]
    ppermute x18, waiting for transfers between devices: 80.4 us -> 85.7 us  [send(): store = {k: lax.ppermute(block, 'chan', [(c, c ^ k) for c in range(chans)])}]
  transfers between devices with their start and end apart: 21 -> 21, of which waited for: 7 -> 8; matrix products, arithmetic and copies ran while one was open for 1% -> 1% of each run, Pallas kernels for 33% -> 31%
where the time goes in v3:
time: 214 us; the launch traced here: 212 us
  waiting for transfers between devices  89.1 us (42%)
  Pallas kernels  82.9 us (39%)
  starting transfers between devices  36.2 us (17%)
  local copies, waits for them, and re-layouts  2.83 us (1%)
    ppermute x18, waiting for transfers between devices, send(): store = {k: lax.ppermute(block, 'chan', [(c, c ^ k) for c in range(chans)])}  85.7 us
    pallas_call x3, Pallas kernels, correlate(): pl.pallas_call(functools.partial(correlate_kernel, (feeds, len(pieces), 1...  50.3 us
    ppermute x18, starting transfers between devices, send(): store = {k: lax.ppermute(block, 'chan', [(c, c ^ k) for c in range(chans)])}  36 us
    pallas_call x2, Pallas kernels, channelize(): pl.pallas_call(functools.partial(channelize_kernel, (feeds, chans, outs_p...  32.6 us
  transfers between devices with their start and end apart: 21, of which 8 were waited for; matrix products, arithmetic and copies ran while one was open for 1% of the time, Pallas kernels for 31%

profile of v3, /device:TPU:0, one launch (start us, length us, event | category | flops | bytes accessed | tf_op | source)
XLA Modules:
  0.0 212.1 jit_solution(13556619533277774507)
XLA Ops:
  0.0 9.7 %shard_map.46 = (bf16[4,2,8,16,128]{4,3,2,1,0:T(8,128)(2,1)}, bf16[4,2,8,16,128]{4,3,2,1,0:T(8,128)(2,1)}, bf16[4,2,8,16,128]{4,3,2,1,0:T(8,128)(2,1)}, bf16[4,2...) custom-call(s32[1]{0:T(128)} %bitcast.1.me_ref, ...), custom_call_target="tpu_custom_call" | custom-call | flops 1610612736 | bytes 10485760 | tf_op jit(solution)/shard_map/pallas_call | solution.py:117
  9.7 3.1 %collective-permute-start = (bf16[4,2,8,16,128]{4,3,2,1,0:T(8,128)(2,1)}, bf16[4,2,8,16,128]{4,3,2,1,0:T(8,128)(2,1)S(1)}, u32[]{:S(2)}, u32[]{:S(2)}) collective-permute-start(bf16[4,2,8,16,128]{4,3,2,1,0:T(8,128)(2,1)} %get-tuple-element.66), channel_id=1, source_target_pairs={{0,4},{2,6},{4,0},{6,2},{8,12},{10,14},{12,8},{14,10},{1,5},{3,7},... | collective-permute-start | bytes 786440 | tf_op jit(solution)/shard_map/ppermute | solution.py:305
  12.8 2.6 %collective-permute-start.2 = (bf16[4,2,8,16,128]{4,3,2,1,0:T(8,128)(2,1)}, bf16[4,2,8,16,128]{4,3,2,1,0:T(8,128)(2,1)S(1)}, u32[]{:S(2)}, u32[]{:S(2)}) collective-permute-start(bf16[4,2,8,16,128]{4,3,2,1,0:T(8,128)(2,1)} %get-tuple-element.72), channel_id=1, source_target_pairs={{0,8},{2,10},{4,12},{6,14},{8,0},{10,2},{12,4},{14,6},{1,9},{3,11}... | collective-permute-start | bytes 786440 | tf_op jit(solution)/shard_map/ppermute | solution.py:305
  15.4 1.5 collective-permute-start.5
  17.2 2.5 %collective-permute-start.7 = (bf16[4,2,8,16,128]{4,3,2,1,0:T(8,128)(2,1)}, bf16[4,2,8,16,128]{4,3,2,1,0:T(8,128)(2,1)S(1)}, u32[]{:S(2)}, u32[]{:S(2)}) collective-permute-start(bf16[4,2,8,16,128]{4,3,2,1,0:T(8,128)(2,1)} %get-tuple-element.89), channel_id=1, source_target_pairs={{0,12},{2,14},{4,8},{6,10},{8,4},{10,6},{12,0},{14,2},{1,13},{3,15... | collective-permute-start | bytes 786440 | tf_op jit(solution)/shard_map/ppermute | solution.py:305
  19.6 23.0 %shard_map.47 = (bf16[4,2,24,16,128]{4,3,2,1,0:T(8,128)(2,1)}, bf16[4,2,24,16,128]{4,3,2,1,0:T(8,128)(2,1)}, bf16[4,2,24,16,128]{4,3,2,1,0:T(8,128)(2,1)}, bf16[...) custom-call(s32[1]{0:T(128)} %bitcast.2.me_ref, ...), custom_call_target="tpu_custom_call" | custom-call | flops 4831838208 | bytes 31457280 | tf_op jit(solution)/shard_map/pallas_call | solution.py:117
  42.7 2.4 %collective-permute-start.8 = (bf16[4,2,8,16,128]{4,3,2,1,0:T(8,128)(2,1)}, bf16[4,2,8,16,128]{4,3,2,1,0:T(8,128)(2,1)S(1)}, u32[]{:S(2)}, u32[]{:S(2)}) collective-permute-start(bf16[4,2,8,16,128]{4,3,2,1,0:T(8,128)(2,1)} %get-tuple-element.92), channel_id=1, source_target_pairs={{0,14},{2,12},{4,10},{6,8},{8,6},{10,4},{12,2},{14,0},{1,15},{3,13... | collective-permute-start | bytes 786440 | tf_op jit(solution)/shard_map/ppermute | solution.py:305
  45.1 1.5 collective-permute-done.6
  46.6 8.3 %collective-permute-done.8 = bf16[4,2,8,16,128]{4,3,2,1,0:T(8,128)(2,1)S(1)} collective-permute-done((bf16[4,2,8,16,128]{4,3,2,1,0:T(8,128)(2,1)}, bf16[4,2,8,16,128]{4,3,2,1,0:T(8,128)(2,1)S(1)}, u32[]{:S(2)}, u32[]{:S(2)}) %collective-permute-start.8) | collective-permute-done | bytes 262176 | tf_op jit(solution)/shard_map/ppermute | solution.py:305
  54.9 3.0 %collective-permute-done.3 = bf16[4,2,8,16,128]{4,3,2,1,0:T(8,128)(2,1)S(1)} collective-permute-done((bf16[4,2,8,16,128]{4,3,2,1,0:T(8,128)(2,1)S(1)}, bf16[4,2,8,16,128]{4,3,2,1,0:T(8,128)(2,1)S(1)}, u32[]{:S(2)}, u32[]{:S(2)}) %collective-permute-start.3) | collective-permute-done | bytes 262176 | tf_op jit(solution)/shard_map/ppermute | solution.py:305
  58.2 6.3 %collective-permute-start.10 = (bf16[3,2,24,16,128]{4,3,2,1,0:T(8,128)(2,1)}, bf16[3,2,24,16,128]{4,3,2,1,0:T(8,128)(2,1)S(1)}, u32[]{:S(2)}, u32[]{:S(2)}) collective-permute-start(bf16[3,2,24,16,128]{4,3,2,1,0:T(8,128)(2,1)} %get-tuple-element.95), channel_id=1, source_target_pairs={{0,8},{2,10},{4,12},{6,14},{8,0},{10,2},{12,4},{14,6},{1,9},{3,11}... | collective-permute-start | bytes 1769480 | tf_op jit(solution)/shard_map/ppermute | solution.py:305
  64.6 1.5 collective-permute-start.1
  67.6 2.1 collective-permute-start.4
  70.2 16.2 %shard_map.48.refs_3_ = f32[2,4,512,1024]{3,2,1,0:T(8,128)} custom-call(s32[1]{0:T(128)} %bitcast.feed_ref, bf16[8,4,2,8,16,128]{5,4,3,2,1,0:T(8,128)(2,1)S(1)} %bitcast_dynamic-update-slice_fusion.8.refs_0_, bf16[8,4,2,8,16,128]{5,4,3,2,1,0:T(8,128)(2,1)} %collective-permute-done.9.refs_1_, bf16[1024,1024]{1,0:T(8,128)(2,1)S(1)} %compare_convert_fusion.refs_2_), custom_call_target="tpu_custom_call" | custom-call | flops 1000 | bytes 1000 | tf_op jit(solution)/shard_map/pallas_call | solution.py:259
  86.4 30.5 %collective-permute-done.10 = bf16[3,2,24,16,128]{4,3,2,1,0:T(8,128)(2,1)S(1)} collective-permute-done((bf16[3,2,24,16,128]{4,3,2,1,0:T(8,128)(2,1)}, bf16[3,2,24,16,128]{4,3,2,1,0:T(8,128)(2,1)S(1)}, u32[]{:S(2)}, u32[]{:S(2)}) %collective-permute-start.10) | collective-permute-done | bytes 589856 | tf_op jit(solution)/shard_map/ppermute | solution.py:305
  117.0 13.6 %collective-permute-done.12 = bf16[3,2,24,16,128]{4,3,2,1,0:T(8,128)(2,1)} collective-permute-done((bf16[3,2,24,16,128]{4,3,2,1,0:T(8,128)(2,1)}, bf16[3,2,24,16,128]{4,3,2,1,0:T(8,128)(2,1)}, u32[]{:S(2)}, u32[]{:S(2)}) %collective-permute-start.12) | collective-permute-done | bytes 589856 | tf_op jit(solution)/shard_map/ppermute | solution.py:305
  132.2 27.4 %collective-permute-done.11 = bf16[4,2,24,16,128]{4,3,2,1,0:T(8,128)(2,1)S(1)} collective-permute-done((bf16[4,2,24,16,128]{4,3,2,1,0:T(8,128)(2,1)S(1)}, bf16[4,2,24,16,128]{4,3,2,1,0:T(8,128)(2,1)S(1)}, u32[]{:S(2)}, u32[]{:S(2)}) %collective-permute-start.11) | collective-permute-done | bytes 786464 | tf_op jit(solution)/shard_map/ppermute | solution.py:305
  161.7 7.0 %collective-permute-start.16 = (bf16[1,2,24,16,128]{4,3,2,1,0:T(8,128)(2,1)S(1)}, bf16[1,2,24,16,128]{4,3,2,1,0:T(8,128)(2,1)S(1)}, u32[]{:S(2)}, u32[]{:S(2)}) collective-permute-start(bf16[1,2,24,16,128]{4,3,2,1,0:T(8,128)(2,1)S(1)} %copy-done.9), channel_id=1, source_target_pairs={{0,8},{2,10},{4,12},{6,14},{8,0},{10,2},{12,4},{14,6},{1,9},{3,11}... | collective-permute-start | bytes 589832 | tf_op jit(solution)/shard_map/ppermute | solution.py:305
  168.7 2.7 %collective-permute-start.18 = (bf16[1,2,24,16,128]{4,3,2,1,0:T(8,128)(2,1)S(1)}, bf16[1,2,24,16,128]{4,3,2,1,0:T(8,128)(2,1)S(1)}, u32[]{:S(2)}, u32[]{:S(2)}) collective-permute-start(bf16[1,2,24,16,128]{4,3,2,1,0:T(8,128)(2,1)S(1)} %copy-done.7), channel_id=1, source_target_pairs={{0,12},{2,14},{4,8},{6,10},{8,4},{10,6},{12,0},{14,2},{1,13},{3,15... | collective-permute-start | bytes 589832 | tf_op jit(solution)/shard_map/ppermute | solution.py:305
  171.4 1.4 collective-permute-start.19
  172.7 25.6 %shard_map.49.refs_3_ = f32[2,4,512,1024]{3,2,1,0:T(8,128)} custom-call(s32[1]{0:T(128)} %bitcast.feed_ref, bf16[8,3,2,24,16,128]{5,4,3,2,1,0:T(8,128)(2,1)S(1)} %bitcast_dynamic-update-slice_fusion.refs_0_, bf16[8,3,2,24,16,128]{5,4,3,2,1,0:T(8,128)(2,1)S(1)} %collective-permute-done.15.refs_1_, ...), custom_call_target="tpu_custom_call", output_to_operand_aliasing={{}: (4, {})} | custom-call | flops 1000 | bytes 1000 | tf_op jit(solution)/shard_map/pallas_call | solution.py:259
  198.5 1.4 collective-permute-done.17
  200.1 3.4 %collective-permute-done.20.refs_1_ = bf16[8,1,2,24,16,128]{5,4,3,2,1,0:T(8,128)(2,1)S(1)} collective-permute-done((bf16[8,1,2,24,16,128]{5,4,3,2,1,0:T(8,128)(2,1)S(1)}, bf16[8,1,2,24,16,128]{5,4,3,2,1,0:T(8,128)(2,1)S(1)}, u32[]{:S(2)}, u32[]{:S(2)}) %collective-permute-start.20) | collective-permute-done | bytes 1572896 | tf_op jit(solution)/shard_map/ppermute | solution.py:318
  203.5 8.5 %shard_map.50 = f32[2,4,512,1024]{3,2,1,0:T(8,128)} custom-call(s32[1]{0:T(128)} %bitcast.feed_ref, bf16[8,1,2,24,16,128]{5,4,3,2,1,0:T(8,128)(2,1)S(1)} %bitcast_dynamic-update-slice_fusion.16.refs_0_, bf16[8,1,2,24,16,128]{5,4,3,2,1,0:T(8,128)(2,1)S(1)} %collective-permute-done.20.refs_1_, ...), custom_call_target="tpu_custom_call", output_to_operand_aliasing={{}: (4, {})} | custom-call | flops 1000 | bytes 1000 | tf_op jit(solution)/shard_map/pallas_call | solution.py:259
  (74 shorter events, 6.6 us)
Async XLA Ops:
  9.7 35.4 %collective-permute-start = (bf16[4,2,8,16,128]{4,3,2,1,0:T(8,128)(2,1)}, bf16[4,2,8,16,128]{4,3,2,1,0:T(8,128)(2,1)S(1)}, u32[]{:S(2)}, u32[]{:S(2)}) collective-permute-start(bf16[4,2,8,16,128]{4,3,2,1,0:T(8,128)(2,1)} %get-tuple-element.66), channel_id=1, source_target_pairs={{0,4},{2,6},{4,0},{6,2},{8,12},{10,14},{12,8},{14,10},{1,5},{3,7},... | collective-permute-start | bytes 786440 | tf_op jit(solution)/shard_map/ppermute | solution.py:305
  12.8 32.3 %collective-permute-start.2 = (bf16[4,2,8,16,128]{4,3,2,1,0:T(8,128)(2,1)}, bf16[4,2,8,16,128]{4,3,2,1,0:T(8,128)(2,1)S(1)}, u32[]{:S(2)}, u32[]{:S(2)}) collective-permute-start(bf16[4,2,8,16,128]{4,3,2,1,0:T(8,128)(2,1)} %get-tuple-element.72), channel_id=1, source_target_pairs={{0,8},{2,10},{4,12},{6,14},{8,0},{10,2},{12,4},{14,6},{1,9},{3,11}... | collective-permute-start | bytes 786440 | tf_op jit(solution)/shard_map/ppermute | solution.py:305
  15.4 27.3 %collective-permute-start.5 = (bf16[4,2,8,16,128]{4,3,2,1,0:T(8,128)(2,1)}, bf16[4,2,8,16,128]{4,3,2,1,0:T(8,128)(2,1)S(1)}, u32[]{:S(2)}, u32[]{:S(2)}) collective-permute-start(bf16[4,2,8,16,128]{4,3,2,1,0:T(8,128)(2,1)} %get-tuple-element.80), channel_id=1, source_target_pairs={{0,2},{2,0},{4,6},{6,4},{8,10},{10,8},{12,14},{14,12},{1,3},{3,1},... | collective-permute-start | bytes 786440 | tf_op jit(solution)/shard_map/ppermute | solution.py:305
  16.9 29.7 %collective-permute-start.6 = (bf16[4,2,8,16,128]{4,3,2,1,0:T(8,128)(2,1)}, bf16[4,2,8,16,128]{4,3,2,1,0:T(8,128)(2,1)S(1)}, u32[]{:S(2)}, u32[]{:S(2)}) collective-permute-start(bf16[4,2,8,16,128]{4,3,2,1,0:T(8,128)(2,1)} %get-tuple-element.86), channel_id=1, source_target_pairs={{0,10},{2,8},{4,14},{6,12},{8,2},{10,0},{12,6},{14,4},{1,11},{3,9}... | collective-permute-start | bytes 786440 | tf_op jit(solution)/shard_map/ppermute | solution.py:305
  17.2 29.4 %collective-permute-start.7 = (bf16[4,2,8,16,128]{4,3,2,1,0:T(8,128)(2,1)}, bf16[4,2,8,16,128]{4,3,2,1,0:T(8,128)(2,1)S(1)}, u32[]{:S(2)}, u32[]{:S(2)}) collective-permute-start(bf16[4,2,8,16,128]{4,3,2,1,0:T(8,128)(2,1)} %get-tuple-element.89), channel_id=1, source_target_pairs={{0,12},{2,14},{4,8},{6,10},{8,4},{10,6},{12,0},{14,2},{1,13},{3,15... | collective-permute-start | bytes 786440 | tf_op jit(solution)/shard_map/ppermute | solution.py:305
  42.7 12.2 %collective-permute-start.8 = (bf16[4,2,8,16,128]{4,3,2,1,0:T(8,128)(2,1)}, bf16[4,2,8,16,128]{4,3,2,1,0:T(8,128)(2,1)S(1)}, u32[]{:S(2)}, u32[]{:S(2)}) collective-permute-start(bf16[4,2,8,16,128]{4,3,2,1,0:T(8,128)(2,1)} %get-tuple-element.92), channel_id=1, source_target_pairs={{0,14},{2,12},{4,10},{6,8},{8,6},{10,4},{12,2},{14,0},{1,15},{3,13... | collective-permute-start | bytes 786440 | tf_op jit(solution)/shard_map/ppermute | solution.py:305
  45.0 12.9 %collective-permute-start.3 = (bf16[4,2,8,16,128]{4,3,2,1,0:T(8,128)(2,1)S(1)}, bf16[4,2,8,16,128]{4,3,2,1,0:T(8,128)(2,1)S(1)}, u32[]{:S(2)}, u32[]{:S(2)}) collective-permute-start(bf16[4,2,8,16,128]{4,3,2,1,0:T(8,128)(2,1)S(1)} %copy-done.5), channel_id=1, source_target_pairs={{0,6},{2,4},{4,2},{6,0},{8,14},{10,12},{12,10},{14,8},{1,7},{3,5},... | collective-permute-start | bytes 786440 | tf_op jit(solution)/shard_map/ppermute | solution.py:305
  58.1 9.5 %collective-permute-start.9 = (bf16[8,4,2,8,16,128]{5,4,3,2,1,0:T(8,128)(2,1)S(1)}, bf16[8,4,2,8,16,128]{5,4,3,2,1,0:T(8,128)(2,1)}, u32[]{:S(2)}, u32[]{:S(2)}) collective-permute-start(bf16[8,4,2,8,16,128]{5,4,3,2,1,0:T(8,128)(2,1)S(1)} %bitcast_dynamic-update-slice_fusion.8.refs_0_), channel_id=1, source_target_pairs={{0,1},{1,0},{2,3},{3,2},{4,5},{5,4},{6,7},{7,6},{8,9},{9,8},{10,11... | collective-permute-start | bytes 6291464 | tf_op jit(solution)/shard_map/ppermute | solution.py:318
  58.2 58.6 %collective-permute-start.10 = (bf16[3,2,24,16,128]{4,3,2,1,0:T(8,128)(2,1)}, bf16[3,2,24,16,128]{4,3,2,1,0:T(8,128)(2,1)S(1)}, u32[]{:S(2)}, u32[]{:S(2)}) collective-permute-start(bf16[3,2,24,16,128]{4,3,2,1,0:T(8,128)(2,1)} %get-tuple-element.95), channel_id=1, source_target_pairs={{0,8},{2,10},{4,12},{6,14},{8,0},{10,2},{12,4},{14,6},{1,9},{3,11}... | collective-permute-start | bytes 1769480 | tf_op jit(solution)/shard_map/ppermute | solution.py:305
  64.6 66.0 %collective-permute-start.1 = (bf16[4,2,24,16,128]{4,3,2,1,0:T(8,128)(2,1)}, bf16[4,2,24,16,128]{4,3,2,1,0:T(8,128)(2,1)S(1)}, u32[]{:S(2)}, u32[]{:S(2)}) collective-permute-start(bf16[4,2,24,16,128]{4,3,2,1,0:T(8,128)(2,1)} %get-tuple-element.67), channel_id=1, source_target_pairs={{0,2},{2,0},{4,6},{6,4},{8,10},{10,8},{12,14},{14,12},{1,3},{3,1},... | collective-permute-start | bytes 2359304 | tf_op jit(solution)/shard_map/ppermute | solution.py:305
  66.1 64.5 %collective-permute-start.12 = (bf16[3,2,24,16,128]{4,3,2,1,0:T(8,128)(2,1)}, bf16[3,2,24,16,128]{4,3,2,1,0:T(8,128)(2,1)}, u32[]{:S(2)}, u32[]{:S(2)}) collective-permute-start(bf16[3,2,24,16,128]{4,3,2,1,0:T(8,128)(2,1)} %get-tuple-element.100), channel_id=1, source_target_pairs={{0,10},{2,8},{4,14},{6,12},{8,2},{10,0},{12,6},{14,4},{1,11},{3,9}... | collective-permute-start | bytes 1769480 | tf_op jit(solution)/shard_map/ppermute | solution.py:305
  66.3 65.7 %collective-permute-start.13 = (bf16[3,2,24,16,128]{4,3,2,1,0:T(8,128)(2,1)}, bf16[3,2,24,16,128]{4,3,2,1,0:T(8,128)(2,1)S(1)}, u32[]{:S(2)}, u32[]{:S(2)}) collective-permute-start(bf16[3,2,24,16,128]{4,3,2,1,0:T(8,128)(2,1)} %get-tuple-element.103), channel_id=1, source_target_pairs={{0,12},{2,14},{4,8},{6,10},{8,4},{10,6},{12,0},{14,2},{1,13},{3,15... | collective-permute-start | bytes 1769480 | tf_op jit(solution)/shard_map/ppermute | solution.py:305
  67.6 64.4 %collective-permute-start.4 = (bf16[4,2,24,16,128]{4,3,2,1,0:T(8,128)(2,1)}, bf16[4,2,24,16,128]{4,3,2,1,0:T(8,128)(2,1)S(1)}, u32[]{:S(2)}, u32[]{:S(2)}) collective-permute-start(bf16[4,2,24,16,128]{4,3,2,1,0:T(8,128)(2,1)} %get-tuple-element.74), channel_id=1, source_target_pairs={{0,4},{2,6},{4,0},{6,2},{8,12},{10,14},{12,8},{14,10},{1,5},{3,7},... | collective-permute-start | bytes 2359304 | tf_op jit(solution)/shard_map/ppermute | solution.py:305
  70.1 46.7 %copy-start.3 = (bf16[4,2,24,16,128]{4,3,2,1,0:T(8,128)(2,1)S(1)}, bf16[4,2,24,16,128]{4,3,2,1,0:T(8,128)(2,1)}, u32[]{:S(2)}) copy-start(bf16[4,2,24,16,128]{4,3,2,1,0:T(8,128)(2,1)} %get-tuple-element.96) | copy-start | bytes 2359300
  70.2 46.7 %copy-start = (bf16[4,2,24,16,128]{4,3,2,1,0:T(8,128)(2,1)S(1)}, bf16[4,2,24,16,128]{4,3,2,1,0:T(8,128)(2,1)}, u32[]{:S(2)}) copy-start(bf16[4,2,24,16,128]{4,3,2,1,0:T(8,128)(2,1)} %get-tuple-element.63) | copy-start | bytes 2359300
  70.2 60.4 %copy-start.4 = (bf16[3,2,24,16,128]{4,3,2,1,0:T(8,128)(2,1)S(1)}, bf16[3,2,24,16,128]{4,3,2,1,0:T(8,128)(2,1)}, u32[]{:S(2)}) copy-start(bf16[3,2,24,16,128]{4,3,2,1,0:T(8,128)(2,1)} %get-tuple-element.105) | copy-start | bytes 1769476
  116.9 42.8 %collective-permute-start.11 = (bf16[4,2,24,16,128]{4,3,2,1,0:T(8,128)(2,1)S(1)}, bf16[4,2,24,16,128]{4,3,2,1,0:T(8,128)(2,1)S(1)}, u32[]{:S(2)}, u32[]{:S(2)}) collective-permute-start(bf16[4,2,24,16,128]{4,3,2,1,0:T(8,128)(2,1)S(1)} %copy-done.3), channel_id=1, source_target_pairs={{0,6},{2,4},{4,2},{6,0},{8,14},{10,12},{12,10},{14,8},{1,7},{3,5},... | collective-permute-start | bytes 2359304 | tf_op jit(solution)/shard_map/ppermute | solution.py:305
  130.6 30.8 %collective-permute-start.14 = (bf16[3,2,24,16,128]{4,3,2,1,0:T(8,128)(2,1)S(1)}, bf16[3,2,24,16,128]{4,3,2,1,0:T(8,128)(2,1)S(1)}, u32[]{:S(2)}, u32[]{:S(2)}) collective-permute-start(bf16[3,2,24,16,128]{4,3,2,1,0:T(8,128)(2,1)S(1)} %copy-done.4), channel_id=1, source_target_pairs={{0,14},{2,12},{4,10},{6,8},{8,6},{10,4},{12,2},{14,0},{1,15},{3,13... | collective-permute-start | bytes 1769480 | tf_op jit(solution)/shard_map/ppermute | solution.py:305
  161.6 11.2 %collective-permute-start.15 = (bf16[8,3,2,24,16,128]{5,4,3,2,1,0:T(8,128)(2,1)S(1)}, bf16[8,3,2,24,16,128]{5,4,3,2,1,0:T(8,128)(2,1)S(1)}, u32[]{:S(2)}, u32[]{:S(2)}) collective-permute-start(bf16[8,3,2,24,16,128]{5,4,3,2,1,0:T(8,128)(2,1)S(1)} %bitcast_dynamic-update-slice_fusion.refs_0_), channel_id=1, source_target_pairs={{0,1},{1,0},{2,3},{3,2},{4,5},{5,4},{6,7},{7,6},{8,9},{9,8},{10,11... | collective-permute-start | bytes 14155784 | tf_op jit(solution)/shard_map/ppermute | solution.py:318
  161.7 36.8 %collective-permute-start.16 = (bf16[1,2,24,16,128]{4,3,2,1,0:T(8,128)(2,1)S(1)}, bf16[1,2,24,16,128]{4,3,2,1,0:T(8,128)(2,1)S(1)}, u32[]{:S(2)}, u32[]{:S(2)}) collective-permute-start(bf16[1,2,24,16,128]{4,3,2,1,0:T(8,128)(2,1)S(1)} %copy-done.9), channel_id=1, source_target_pairs={{0,8},{2,10},{4,12},{6,14},{8,0},{10,2},{12,4},{14,6},{1,9},{3,11}... | collective-permute-start | bytes 589832 | tf_op jit(solution)/shard_map/ppermute | solution.py:305
  168.7 31.2 %collective-permute-start.18 = (bf16[1,2,24,16,128]{4,3,2,1,0:T(8,128)(2,1)S(1)}, bf16[1,2,24,16,128]{4,3,2,1,0:T(8,128)(2,1)S(1)}, u32[]{:S(2)}, u32[]{:S(2)}) collective-permute-start(bf16[1,2,24,16,128]{4,3,2,1,0:T(8,128)(2,1)S(1)} %copy-done.7), channel_id=1, source_target_pairs={{0,12},{2,14},{4,8},{6,10},{8,4},{10,6},{12,0},{14,2},{1,13},{3,15... | collective-permute-start | bytes 589832 | tf_op jit(solution)/shard_map/ppermute | solution.py:305
  171.4 28.5 %collective-permute-start.17 = (bf16[1,2,24,16,128]{4,3,2,1,0:T(8,128)(2,1)S(1)}, bf16[1,2,24,16,128]{4,3,2,1,0:T(8,128)(2,1)S(1)}, u32[]{:S(2)}, u32[]{:S(2)}) collective-permute-start(bf16[1,2,24,16,128]{4,3,2,1,0:T(8,128)(2,1)S(1)} %copy-done.8), channel_id=1, source_target_pairs={{0,10},{2,8},{4,14},{6,12},{8,2},{10,0},{12,6},{14,4},{1,11},{3,9}... | collective-permute-start | bytes 589832 | tf_op jit(solution)/shard_map/ppermute | solution.py:305
  171.4 28.6 %collective-permute-start.19 = (bf16[1,2,24,16,128]{4,3,2,1,0:T(8,128)(2,1)S(1)}, bf16[1,2,24,16,128]{4,3,2,1,0:T(8,128)(2,1)S(1)}, u32[]{:S(2)}, u32[]{:S(2)}) collective-permute-start(bf16[1,2,24,16,128]{4,3,2,1,0:T(8,128)(2,1)S(1)} %copy-done.6), channel_id=1, source_target_pairs={{0,14},{2,12},{4,10},{6,8},{8,6},{10,4},{12,2},{14,0},{1,15},{3,13... | collective-permute-start | bytes 589832 | tf_op jit(solution)/shard_map/ppermute | solution.py:305
  200.0 3.5 %collective-permute-start.20 = (bf16[8,1,2,24,16,128]{5,4,3,2,1,0:T(8,128)(2,1)S(1)}, bf16[8,1,2,24,16,128]{5,4,3,2,1,0:T(8,128)(2,1)S(1)}, u32[]{:S(2)}, u32[]{:S(2)}) collective-permute-start(bf16[8,1,2,24,16,128]{5,4,3,2,1,0:T(8,128)(2,1)S(1)} %bitcast_dynamic-update-slice_fusion.16.refs_0_), channel_id=1, source_target_pairs={{0,1},{1,0},{2,3},{3,2},{4,5},{5,4},{6,7},{7,6},{8,9},{9,8},{10,11... | collective-permute-start | bytes 4718600 | tf_op jit(solution)/shard_map/ppermute | solution.py:318
  (7 other events, 108.8 us)

commit v4 on v3

--- a/solution.py
+++ b/solution.py
@@ -206,8 +206,9 @@
 
     half = out_ref.shape[2]
     mine = pl.ds(pl.multiple_of(feed_ref[0] * half, half), half)
-    start = pl.multiple_of(pl.program_id(1) * COLS, COLS)
-    other = pl.ds(start, COLS)
+    cols = out_ref.shape[3]
+    start = pl.multiple_of(pl.program_id(1) * cols, cols)
+    other = pl.ds(start, cols)
 
     def dot(left, right):
         return lax.dot_general(left, right, NT, preferred_element_type=jnp.float32)
@@ -246,8 +247,9 @@
     in_specs.append(
         pl.BlockSpec(select.shape, lambda o, n, feed: (0, 0), pipeline_mode=pl.Buffered(1))
     )
-    out_spec = pl.BlockSpec((2, 1, half, COLS), lambda o, n, feed: (0, first + o, 0, n))
     copies = adds and count == 1
+    cols = COLS // 2 if copies else COLS
+    out_spec = pl.BlockSpec((2, 1, half, cols), lambda o, n, feed: (0, first + o, 0, n))
     aliases = {}
     if result is not None:
         aliases = {1 + len(operands): 0}
@@ -262,7 +264,7 @@
         ),
         grid_spec=pltpu.PrefetchScalarGridSpec(
             num_scalar_prefetch=1,
-            grid=(count, total // COLS),
+            grid=(count, total // cols),
             in_specs=in_specs,
             out_specs=out_spec,
             scratch_shapes=scratch,

time: 214 us -> 214 us (level)
  no operation moved by 1% of the time
where the time goes in v4:
time: 214 us; the launch traced here: 212 us
  waiting for transfers between devices  89.1 us (42%)
  Pallas kernels  83 us (39%)
  starting transfers between devices  36.2 us (17%)
  local copies, waits for them, and re-layouts  2.83 us (1%)
    ppermute x18, waiting for transfers between devices, send(): store = {k: lax.ppermute(block, 'chan', [(c, c ^ k) for c in range(chans)])}  85.7 us
    pallas_call x3, Pallas kernels, correlate(): pl.pallas_call(functools.partial(correlate_kernel, (feeds, len(pieces), 1...  50.4 us
    ppermute x18, starting transfers between devices, send(): store = {k: lax.ppermute(block, 'chan', [(c, c ^ k) for c in range(chans)])}  36 us
    pallas_call x2, Pallas kernels, channelize(): pl.pallas_call(functools.partial(channelize_kernel, (feeds, chans, outs_p...  32.6 us
  transfers between devices with their start and end apart: 21, of which 8 were waited for; matrix products, arithmetic and copies ran while one was open for 1% of the time, Pallas kernels for 31%

profile of v4, /device:TPU:0, one launch (start us, length us, event | category | flops | bytes accessed | tf_op | source)
XLA Modules:
  0.0 212.2 jit_solution(14227892344981142457)
XLA Ops:
  0.0 9.7 %shard_map.46 = (bf16[4,2,8,16,128]{4,3,2,1,0:T(8,128)(2,1)}, bf16[4,2,8,16,128]{4,3,2,1,0:T(8,128)(2,1)}, bf16[4,2,8,16,128]{4,3,2,1,0:T(8,128)(2,1)}, bf16[4,2...) custom-call(s32[1]{0:T(128)} %bitcast.1.me_ref, ...), custom_call_target="tpu_custom_call" | custom-call | flops 1610612736 | bytes 10485760 | tf_op jit(solution)/shard_map/pallas_call | solution.py:117
  9.7 3.1 %collective-permute-start = (bf16[4,2,8,16,128]{4,3,2,1,0:T(8,128)(2,1)}, bf16[4,2,8,16,128]{4,3,2,1,0:T(8,128)(2,1)S(1)}, u32[]{:S(2)}, u32[]{:S(2)}) collective-permute-start(bf16[4,2,8,16,128]{4,3,2,1,0:T(8,128)(2,1)} %get-tuple-element.66), channel_id=1, source_target_pairs={{0,4},{2,6},{4,0},{6,2},{8,12},{10,14},{12,8},{14,10},{1,5},{3,7},... | collective-permute-start | bytes 786440 | tf_op jit(solution)/shard_map/ppermute | solution.py:307
  12.8 2.6 %collective-permute-start.2 = (bf16[4,2,8,16,128]{4,3,2,1,0:T(8,128)(2,1)}, bf16[4,2,8,16,128]{4,3,2,1,0:T(8,128)(2,1)S(1)}, u32[]{:S(2)}, u32[]{:S(2)}) collective-permute-start(bf16[4,2,8,16,128]{4,3,2,1,0:T(8,128)(2,1)} %get-tuple-element.72), channel_id=1, source_target_pairs={{0,8},{2,10},{4,12},{6,14},{8,0},{10,2},{12,4},{14,6},{1,9},{3,11}... | collective-permute-start | bytes 786440 | tf_op jit(solution)/shard_map/ppermute | solution.py:307
  15.4 1.5 collective-permute-start.5
  17.2 2.5 %collective-permute-start.7 = (bf16[4,2,8,16,128]{4,3,2,1,0:T(8,128)(2,1)}, bf16[4,2,8,16,128]{4,3,2,1,0:T(8,128)(2,1)S(1)}, u32[]{:S(2)}, u32[]{:S(2)}) collective-permute-start(bf16[4,2,8,16,128]{4,3,2,1,0:T(8,128)(2,1)} %get-tuple-element.89), channel_id=1, source_target_pairs={{0,12},{2,14},{4,8},{6,10},{8,4},{10,6},{12,0},{14,2},{1,13},{3,15... | collective-permute-start | bytes 786440 | tf_op jit(solution)/shard_map/ppermute | solution.py:307
  19.6 23.0 %shard_map.47 = (bf16[4,2,24,16,128]{4,3,2,1,0:T(8,128)(2,1)}, bf16[4,2,24,16,128]{4,3,2,1,0:T(8,128)(2,1)}, bf16[4,2,24,16,128]{4,3,2,1,0:T(8,128)(2,1)}, bf16[...) custom-call(s32[1]{0:T(128)} %bitcast.2.me_ref, ...), custom_call_target="tpu_custom_call" | custom-call | flops 4831838208 | bytes 31457280 | tf_op jit(solution)/shard_map/pallas_call | solution.py:117
  42.7 2.4 %collective-permute-start.8 = (bf16[4,2,8,16,128]{4,3,2,1,0:T(8,128)(2,1)}, bf16[4,2,8,16,128]{4,3,2,1,0:T(8,128)(2,1)S(1)}, u32[]{:S(2)}, u32[]{:S(2)}) collective-permute-start(bf16[4,2,8,16,128]{4,3,2,1,0:T(8,128)(2,1)} %get-tuple-element.92), channel_id=1, source_target_pairs={{0,14},{2,12},{4,10},{6,8},{8,6},{10,4},{12,2},{14,0},{1,15},{3,13... | collective-permute-start | bytes 786440 | tf_op jit(solution)/shard_map/ppermute | solution.py:307
  45.1 1.5 collective-permute-done.6
  46.6 8.3 %collective-permute-done.8 = bf16[4,2,8,16,128]{4,3,2,1,0:T(8,128)(2,1)S(1)} collective-permute-done((bf16[4,2,8,16,128]{4,3,2,1,0:T(8,128)(2,1)}, bf16[4,2,8,16,128]{4,3,2,1,0:T(8,128)(2,1)S(1)}, u32[]{:S(2)}, u32[]{:S(2)}) %collective-permute-start.8) | collective-permute-done | bytes 262176 | tf_op jit(solution)/shard_map/ppermute | solution.py:307
  54.9 3.0 %collective-permute-done.3 = bf16[4,2,8,16,128]{4,3,2,1,0:T(8,128)(2,1)S(1)} collective-permute-done((bf16[4,2,8,16,128]{4,3,2,1,0:T(8,128)(2,1)S(1)}, bf16[4,2,8,16,128]{4,3,2,1,0:T(8,128)(2,1)S(1)}, u32[]{:S(2)}, u32[]{:S(2)}) %collective-permute-start.3) | collective-permute-done | bytes 262176 | tf_op jit(solution)/shard_map/ppermute | solution.py:307
  58.2 6.3 %collective-permute-start.10 = (bf16[3,2,24,16,128]{4,3,2,1,0:T(8,128)(2,1)}, bf16[3,2,24,16,128]{4,3,2,1,0:T(8,128)(2,1)S(1)}, u32[]{:S(2)}, u32[]{:S(2)}) collective-permute-start(bf16[3,2,24,16,128]{4,3,2,1,0:T(8,128)(2,1)} %get-tuple-element.95), channel_id=1, source_target_pairs={{0,8},{2,10},{4,12},{6,14},{8,0},{10,2},{12,4},{14,6},{1,9},{3,11}... | collective-permute-start | bytes 1769480 | tf_op jit(solution)/shard_map/ppermute | solution.py:307
  64.6 1.5 collective-permute-start.1
  67.6 2.1 collective-permute-start.4
  70.2 16.2 %shard_map.48.refs_3_ = f32[2,4,512,1024]{3,2,1,0:T(8,128)} custom-call(s32[1]{0:T(128)} %bitcast.feed_ref, bf16[8,4,2,8,16,128]{5,4,3,2,1,0:T(8,128)(2,1)S(1)} %bitcast_dynamic-update-slice_fusion.8.refs_0_, bf16[8,4,2,8,16,128]{5,4,3,2,1,0:T(8,128)(2,1)} %collective-permute-done.9.refs_1_, bf16[1024,1024]{1,0:T(8,128)(2,1)S(1)} %compare_convert_fusion.refs_2_), custom_call_target="tpu_custom_call" | custom-call | flops 1000 | bytes 1000 | tf_op jit(solution)/shard_map/pallas_call | solution.py:261
  86.4 30.5 %collective-permute-done.10 = bf16[3,2,24,16,128]{4,3,2,1,0:T(8,128)(2,1)S(1)} collective-permute-done((bf16[3,2,24,16,128]{4,3,2,1,0:T(8,128)(2,1)}, bf16[3,2,24,16,128]{4,3,2,1,0:T(8,128)(2,1)S(1)}, u32[]{:S(2)}, u32[]{:S(2)}) %collective-permute-start.10) | collective-permute-done | bytes 589856 | tf_op jit(solution)/shard_map/ppermute | solution.py:307
  117.0 13.6 %collective-permute-done.12 = bf16[3,2,24,16,128]{4,3,2,1,0:T(8,128)(2,1)} collective-permute-done((bf16[3,2,24,16,128]{4,3,2,1,0:T(8,128)(2,1)}, bf16[3,2,24,16,128]{4,3,2,1,0:T(8,128)(2,1)}, u32[]{:S(2)}, u32[]{:S(2)}) %collective-permute-start.12) | collective-permute-done | bytes 589856 | tf_op jit(solution)/shard_map/ppermute | solution.py:307
  132.2 27.4 %collective-permute-done.11 = bf16[4,2,24,16,128]{4,3,2,1,0:T(8,128)(2,1)S(1)} collective-permute-done((bf16[4,2,24,16,128]{4,3,2,1,0:T(8,128)(2,1)S(1)}, bf16[4,2,24,16,128]{4,3,2,1,0:T(8,128)(2,1)S(1)}, u32[]{:S(2)}, u32[]{:S(2)}) %collective-permute-start.11) | collective-permute-done | bytes 786464 | tf_op jit(solution)/shard_map/ppermute | solution.py:307
  161.7 7.0 %collective-permute-start.16 = (bf16[1,2,24,16,128]{4,3,2,1,0:T(8,128)(2,1)S(1)}, bf16[1,2,24,16,128]{4,3,2,1,0:T(8,128)(2,1)S(1)}, u32[]{:S(2)}, u32[]{:S(2)}) collective-permute-start(bf16[1,2,24,16,128]{4,3,2,1,0:T(8,128)(2,1)S(1)} %copy-done.9), channel_id=1, source_target_pairs={{0,8},{2,10},{4,12},{6,14},{8,0},{10,2},{12,4},{14,6},{1,9},{3,11}... | collective-permute-start | bytes 589832 | tf_op jit(solution)/shard_map/ppermute | solution.py:307
  168.7 2.7 %collective-permute-start.18 = (bf16[1,2,24,16,128]{4,3,2,1,0:T(8,128)(2,1)S(1)}, bf16[1,2,24,16,128]{4,3,2,1,0:T(8,128)(2,1)S(1)}, u32[]{:S(2)}, u32[]{:S(2)}) collective-permute-start(bf16[1,2,24,16,128]{4,3,2,1,0:T(8,128)(2,1)S(1)} %copy-done.7), channel_id=1, source_target_pairs={{0,12},{2,14},{4,8},{6,10},{8,4},{10,6},{12,0},{14,2},{1,13},{3,15... | collective-permute-start | bytes 589832 | tf_op jit(solution)/shard_map/ppermute | solution.py:307
  171.4 1.4 collective-permute-start.19
  172.7 25.6 %shard_map.49.refs_3_ = f32[2,4,512,1024]{3,2,1,0:T(8,128)} custom-call(s32[1]{0:T(128)} %bitcast.feed_ref, bf16[8,3,2,24,16,128]{5,4,3,2,1,0:T(8,128)(2,1)S(1)} %bitcast_dynamic-update-slice_fusion.refs_0_, bf16[8,3,2,24,16,128]{5,4,3,2,1,0:T(8,128)(2,1)S(1)} %collective-permute-done.15.refs_1_, ...), custom_call_target="tpu_custom_call", output_to_operand_aliasing={{}: (4, {})} | custom-call | flops 1000 | bytes 1000 | tf_op jit(solution)/shard_map/pallas_call | solution.py:261
  198.5 1.4 collective-permute-done.17
  200.1 3.4 %collective-permute-done.20.refs_1_ = bf16[8,1,2,24,16,128]{5,4,3,2,1,0:T(8,128)(2,1)S(1)} collective-permute-done((bf16[8,1,2,24,16,128]{5,4,3,2,1,0:T(8,128)(2,1)S(1)}, bf16[8,1,2,24,16,128]{5,4,3,2,1,0:T(8,128)(2,1)S(1)}, u32[]{:S(2)}, u32[]{:S(2)}) %collective-permute-start.20) | collective-permute-done | bytes 1572896 | tf_op jit(solution)/shard_map/ppermute | solution.py:320
  203.5 8.6 %shard_map.50 = f32[2,4,512,1024]{3,2,1,0:T(8,128)} custom-call(s32[1]{0:T(128)} %bitcast.feed_ref, bf16[8,1,2,24,16,128]{5,4,3,2,1,0:T(8,128)(2,1)S(1)} %bitcast_dynamic-update-slice_fusion.16.refs_0_, bf16[8,1,2,24,16,128]{5,4,3,2,1,0:T(8,128)(2,1)S(1)} %collective-permute-done.20.refs_1_, ...), custom_call_target="tpu_custom_call", output_to_operand_aliasing={{}: (4, {})} | custom-call | flops 1000 | bytes 1000 | tf_op jit(solution)/shard_map/pallas_call | solution.py:261
  (74 shorter events, 6.6 us)
Async XLA Ops:
  9.7 35.4 %collective-permute-start = (bf16[4,2,8,16,128]{4,3,2,1,0:T(8,128)(2,1)}, bf16[4,2,8,16,128]{4,3,2,1,0:T(8,128)(2,1)S(1)}, u32[]{:S(2)}, u32[]{:S(2)}) collective-permute-start(bf16[4,2,8,16,128]{4,3,2,1,0:T(8,128)(2,1)} %get-tuple-element.66), channel_id=1, source_target_pairs={{0,4},{2,6},{4,0},{6,2},{8,12},{10,14},{12,8},{14,10},{1,5},{3,7},... | collective-permute-start | bytes 786440 | tf_op jit(solution)/shard_map/ppermute | solution.py:307
  12.8 32.3 %collective-permute-start.2 = (bf16[4,2,8,16,128]{4,3,2,1,0:T(8,128)(2,1)}, bf16[4,2,8,16,128]{4,3,2,1,0:T(8,128)(2,1)S(1)}, u32[]{:S(2)}, u32[]{:S(2)}) collective-permute-start(bf16[4,2,8,16,128]{4,3,2,1,0:T(8,128)(2,1)} %get-tuple-element.72), channel_id=1, source_target_pairs={{0,8},{2,10},{4,12},{6,14},{8,0},{10,2},{12,4},{14,6},{1,9},{3,11}... | collective-permute-start | bytes 786440 | tf_op jit(solution)/shard_map/ppermute | solution.py:307
  15.4 27.3 %collective-permute-start.5 = (bf16[4,2,8,16,128]{4,3,2,1,0:T(8,128)(2,1)}, bf16[4,2,8,16,128]{4,3,2,1,0:T(8,128)(2,1)S(1)}, u32[]{:S(2)}, u32[]{:S(2)}) collective-permute-start(bf16[4,2,8,16,128]{4,3,2,1,0:T(8,128)(2,1)} %get-tuple-element.80), channel_id=1, source_target_pairs={{0,2},{2,0},{4,6},{6,4},{8,10},{10,8},{12,14},{14,12},{1,3},{3,1},... | collective-permute-start | bytes 786440 | tf_op jit(solution)/shard_map/ppermute | solution.py:307
  16.9 29.7 %collective-permute-start.6 = (bf16[4,2,8,16,128]{4,3,2,1,0:T(8,128)(2,1)}, bf16[4,2,8,16,128]{4,3,2,1,0:T(8,128)(2,1)S(1)}, u32[]{:S(2)}, u32[]{:S(2)}) collective-permute-start(bf16[4,2,8,16,128]{4,3,2,1,0:T(8,128)(2,1)} %get-tuple-element.86), channel_id=1, source_target_pairs={{0,10},{2,8},{4,14},{6,12},{8,2},{10,0},{12,6},{14,4},{1,11},{3,9}... | collective-permute-start | bytes 786440 | tf_op jit(solution)/shard_map/ppermute | solution.py:307
  17.2 29.4 %collective-permute-start.7 = (bf16[4,2,8,16,128]{4,3,2,1,0:T(8,128)(2,1)}, bf16[4,2,8,16,128]{4,3,2,1,0:T(8,128)(2,1)S(1)}, u32[]{:S(2)}, u32[]{:S(2)}) collective-permute-start(bf16[4,2,8,16,128]{4,3,2,1,0:T(8,128)(2,1)} %get-tuple-element.89), channel_id=1, source_target_pairs={{0,12},{2,14},{4,8},{6,10},{8,4},{10,6},{12,0},{14,2},{1,13},{3,15... | collective-permute-start | bytes 786440 | tf_op jit(solution)/shard_map/ppermute | solution.py:307
  42.7 12.2 %collective-permute-start.8 = (bf16[4,2,8,16,128]{4,3,2,1,0:T(8,128)(2,1)}, bf16[4,2,8,16,128]{4,3,2,1,0:T(8,128)(2,1)S(1)}, u32[]{:S(2)}, u32[]{:S(2)}) collective-permute-start(bf16[4,2,8,16,128]{4,3,2,1,0:T(8,128)(2,1)} %get-tuple-element.92), channel_id=1, source_target_pairs={{0,14},{2,12},{4,10},{6,8},{8,6},{10,4},{12,2},{14,0},{1,15},{3,13... | collective-permute-start | bytes 786440 | tf_op jit(solution)/shard_map/ppermute | solution.py:307
  45.0 12.9 %collective-permute-start.3 = (bf16[4,2,8,16,128]{4,3,2,1,0:T(8,128)(2,1)S(1)}, bf16[4,2,8,16,128]{4,3,2,1,0:T(8,128)(2,1)S(1)}, u32[]{:S(2)}, u32[]{:S(2)}) collective-permute-start(bf16[4,2,8,16,128]{4,3,2,1,0:T(8,128)(2,1)S(1)} %copy-done.5), channel_id=1, source_target_pairs={{0,6},{2,4},{4,2},{6,0},{8,14},{10,12},{12,10},{14,8},{1,7},{3,5},... | collective-permute-start | bytes 786440 | tf_op jit(solution)/shard_map/ppermute | solution.py:307
  58.1 9.5 %collective-permute-start.9 = (bf16[8,4,2,8,16,128]{5,4,3,2,1,0:T(8,128)(2,1)S(1)}, bf16[8,4,2,8,16,128]{5,4,3,2,1,0:T(8,128)(2,1)}, u32[]{:S(2)}, u32[]{:S(2)}) collective-permute-start(bf16[8,4,2,8,16,128]{5,4,3,2,1,0:T(8,128)(2,1)S(1)} %bitcast_dynamic-update-slice_fusion.8.refs_0_), channel_id=1, source_target_pairs={{0,1},{1,0},{2,3},{3,2},{4,5},{5,4},{6,7},{7,6},{8,9},{9,8},{10,11... | collective-permute-start | bytes 6291464 | tf_op jit(solution)/shard_map/ppermute | solution.py:320
  58.2 58.6 %collective-permute-start.10 = (bf16[3,2,24,16,128]{4,3,2,1,0:T(8,128)(2,1)}, bf16[3,2,24,16,128]{4,3,2,1,0:T(8,128)(2,1)S(1)}, u32[]{:S(2)}, u32[]{:S(2)}) collective-permute-start(bf16[3,2,24,16,128]{4,3,2,1,0:T(8,128)(2,1)} %get-tuple-element.95), channel_id=1, source_target_pairs={{0,8},{2,10},{4,12},{6,14},{8,0},{10,2},{12,4},{14,6},{1,9},{3,11}... | collective-permute-start | bytes 1769480 | tf_op jit(solution)/shard_map/ppermute | solution.py:307
  64.6 66.0 %collective-permute-start.1 = (bf16[4,2,24,16,128]{4,3,2,1,0:T(8,128)(2,1)}, bf16[4,2,24,16,128]{4,3,2,1,0:T(8,128)(2,1)S(1)}, u32[]{:S(2)}, u32[]{:S(2)}) collective-permute-start(bf16[4,2,24,16,128]{4,3,2,1,0:T(8,128)(2,1)} %get-tuple-element.67), channel_id=1, source_target_pairs={{0,2},{2,0},{4,6},{6,4},{8,10},{10,8},{12,14},{14,12},{1,3},{3,1},... | collective-permute-start | bytes 2359304 | tf_op jit(solution)/shard_map/ppermute | solution.py:307
  66.1 64.5 %collective-permute-start.12 = (bf16[3,2,24,16,128]{4,3,2,1,0:T(8,128)(2,1)}, bf16[3,2,24,16,128]{4,3,2,1,0:T(8,128)(2,1)}, u32[]{:S(2)}, u32[]{:S(2)}) collective-permute-start(bf16[3,2,24,16,128]{4,3,2,1,0:T(8,128)(2,1)} %get-tuple-element.100), channel_id=1, source_target_pairs={{0,10},{2,8},{4,14},{6,12},{8,2},{10,0},{12,6},{14,4},{1,11},{3,9}... | collective-permute-start | bytes 1769480 | tf_op jit(solution)/shard_map/ppermute | solution.py:307
  66.3 65.7 %collective-permute-start.13 = (bf16[3,2,24,16,128]{4,3,2,1,0:T(8,128)(2,1)}, bf16[3,2,24,16,128]{4,3,2,1,0:T(8,128)(2,1)S(1)}, u32[]{:S(2)}, u32[]{:S(2)}) collective-permute-start(bf16[3,2,24,16,128]{4,3,2,1,0:T(8,128)(2,1)} %get-tuple-element.103), channel_id=1, source_target_pairs={{0,12},{2,14},{4,8},{6,10},{8,4},{10,6},{12,0},{14,2},{1,13},{3,15... | collective-permute-start | bytes 1769480 | tf_op jit(solution)/shard_map/ppermute | solution.py:307
  67.6 64.4 %collective-permute-start.4 = (bf16[4,2,24,16,128]{4,3,2,1,0:T(8,128)(2,1)}, bf16[4,2,24,16,128]{4,3,2,1,0:T(8,128)(2,1)S(1)}, u32[]{:S(2)}, u32[]{:S(2)}) collective-permute-start(bf16[4,2,24,16,128]{4,3,2,1,0:T(8,128)(2,1)} %get-tuple-element.74), channel_id=1, source_target_pairs={{0,4},{2,6},{4,0},{6,2},{8,12},{10,14},{12,8},{14,10},{1,5},{3,7},... | collective-permute-start | bytes 2359304 | tf_op jit(solution)/shard_map/ppermute | solution.py:307
  70.1 46.7 %copy-start.3 = (bf16[4,2,24,16,128]{4,3,2,1,0:T(8,128)(2,1)S(1)}, bf16[4,2,24,16,128]{4,3,2,1,0:T(8,128)(2,1)}, u32[]{:S(2)}) copy-start(bf16[4,2,24,16,128]{4,3,2,1,0:T(8,128)(2,1)} %get-tuple-element.96) | copy-start | bytes 2359300
  70.2 46.7 %copy-start = (bf16[4,2,24,16,128]{4,3,2,1,0:T(8,128)(2,1)S(1)}, bf16[4,2,24,16,128]{4,3,2,1,0:T(8,128)(2,1)}, u32[]{:S(2)}) copy-start(bf16[4,2,24,16,128]{4,3,2,1,0:T(8,128)(2,1)} %get-tuple-element.63) | copy-start | bytes 2359300
  70.2 60.4 %copy-start.4 = (bf16[3,2,24,16,128]{4,3,2,1,0:T(8,128)(2,1)S(1)}, bf16[3,2,24,16,128]{4,3,2,1,0:T(8,128)(2,1)}, u32[]{:S(2)}) copy-start(bf16[3,2,24,16,128]{4,3,2,1,0:T(8,128)(2,1)} %get-tuple-element.105) | copy-start | bytes 1769476
  116.9 42.8 %collective-permute-start.11 = (bf16[4,2,24,16,128]{4,3,2,1,0:T(8,128)(2,1)S(1)}, bf16[4,2,24,16,128]{4,3,2,1,0:T(8,128)(2,1)S(1)}, u32[]{:S(2)}, u32[]{:S(2)}) collective-permute-start(bf16[4,2,24,16,128]{4,3,2,1,0:T(8,128)(2,1)S(1)} %copy-done.3), channel_id=1, source_target_pairs={{0,6},{2,4},{4,2},{6,0},{8,14},{10,12},{12,10},{14,8},{1,7},{3,5},... | collective-permute-start | bytes 2359304 | tf_op jit(solution)/shard_map/ppermute | solution.py:307
  130.6 30.8 %collective-permute-start.14 = (bf16[3,2,24,16,128]{4,3,2,1,0:T(8,128)(2,1)S(1)}, bf16[3,2,24,16,128]{4,3,2,1,0:T(8,128)(2,1)S(1)}, u32[]{:S(2)}, u32[]{:S(2)}) collective-permute-start(bf16[3,2,24,16,128]{4,3,2,1,0:T(8,128)(2,1)S(1)} %copy-done.4), channel_id=1, source_target_pairs={{0,14},{2,12},{4,10},{6,8},{8,6},{10,4},{12,2},{14,0},{1,15},{3,13... | collective-permute-start | bytes 1769480 | tf_op jit(solution)/shard_map/ppermute | solution.py:307
  161.6 11.2 %collective-permute-start.15 = (bf16[8,3,2,24,16,128]{5,4,3,2,1,0:T(8,128)(2,1)S(1)}, bf16[8,3,2,24,16,128]{5,4,3,2,1,0:T(8,128)(2,1)S(1)}, u32[]{:S(2)}, u32[]{:S(2)}) collective-permute-start(bf16[8,3,2,24,16,128]{5,4,3,2,1,0:T(8,128)(2,1)S(1)} %bitcast_dynamic-update-slice_fusion.refs_0_), channel_id=1, source_target_pairs={{0,1},{1,0},{2,3},{3,2},{4,5},{5,4},{6,7},{7,6},{8,9},{9,8},{10,11... | collective-permute-start | bytes 14155784 | tf_op jit(solution)/shard_map/ppermute | solution.py:320
  161.7 36.8 %collective-permute-start.16 = (bf16[1,2,24,16,128]{4,3,2,1,0:T(8,128)(2,1)S(1)}, bf16[1,2,24,16,128]{4,3,2,1,0:T(8,128)(2,1)S(1)}, u32[]{:S(2)}, u32[]{:S(2)}) collective-permute-start(bf16[1,2,24,16,128]{4,3,2,1,0:T(8,128)(2,1)S(1)} %copy-done.9), channel_id=1, source_target_pairs={{0,8},{2,10},{4,12},{6,14},{8,0},{10,2},{12,4},{14,6},{1,9},{3,11}... | collective-permute-start | bytes 589832 | tf_op jit(solution)/shard_map/ppermute | solution.py:307
  168.7 31.2 %collective-permute-start.18 = (bf16[1,2,24,16,128]{4,3,2,1,0:T(8,128)(2,1)S(1)}, bf16[1,2,24,16,128]{4,3,2,1,0:T(8,128)(2,1)S(1)}, u32[]{:S(2)}, u32[]{:S(2)}) collective-permute-start(bf16[1,2,24,16,128]{4,3,2,1,0:T(8,128)(2,1)S(1)} %copy-done.7), channel_id=1, source_target_pairs={{0,12},{2,14},{4,8},{6,10},{8,4},{10,6},{12,0},{14,2},{1,13},{3,15... | collective-permute-start | bytes 589832 | tf_op jit(solution)/shard_map/ppermute | solution.py:307
  171.4 28.5 %collective-permute-start.17 = (bf16[1,2,24,16,128]{4,3,2,1,0:T(8,128)(2,1)S(1)}, bf16[1,2,24,16,128]{4,3,2,1,0:T(8,128)(2,1)S(1)}, u32[]{:S(2)}, u32[]{:S(2)}) collective-permute-start(bf16[1,2,24,16,128]{4,3,2,1,0:T(8,128)(2,1)S(1)} %copy-done.8), channel_id=1, source_target_pairs={{0,10},{2,8},{4,14},{6,12},{8,2},{10,0},{12,6},{14,4},{1,11},{3,9}... | collective-permute-start | bytes 589832 | tf_op jit(solution)/shard_map/ppermute | solution.py:307
  171.4 28.6 %collective-permute-start.19 = (bf16[1,2,24,16,128]{4,3,2,1,0:T(8,128)(2,1)S(1)}, bf16[1,2,24,16,128]{4,3,2,1,0:T(8,128)(2,1)S(1)}, u32[]{:S(2)}, u32[]{:S(2)}) collective-permute-start(bf16[1,2,24,16,128]{4,3,2,1,0:T(8,128)(2,1)S(1)} %copy-done.6), channel_id=1, source_target_pairs={{0,14},{2,12},{4,10},{6,8},{8,6},{10,4},{12,2},{14,0},{1,15},{3,13... | collective-permute-start | bytes 589832 | tf_op jit(solution)/shard_map/ppermute | solution.py:307
  200.0 3.5 %collective-permute-start.20 = (bf16[8,1,2,24,16,128]{5,4,3,2,1,0:T(8,128)(2,1)S(1)}, bf16[8,1,2,24,16,128]{5,4,3,2,1,0:T(8,128)(2,1)S(1)}, u32[]{:S(2)}, u32[]{:S(2)}) collective-permute-start(bf16[8,1,2,24,16,128]{5,4,3,2,1,0:T(8,128)(2,1)S(1)} %bitcast_dynamic-update-slice_fusion.16.refs_0_), channel_id=1, source_target_pairs={{0,1},{1,0},{2,3},{3,2},{4,5},{5,4},{6,7},{7,6},{8,9},{9,8},{10,11... | collective-permute-start | bytes 4718600 | tf_op jit(solution)/shard_map/ppermute | solution.py:320
  (7 other events, 108.8 us)
